TPU v7x, 32 devices: a whole 2x2x4 slice. The times are simulated.
32 devices in a mesh: case: 2 (over x), box: 16 (over z, y, core).
Axes of the slice: x: 2, y: 2, z: 4, core: 2. Of those that a mesh axis runs over, the one named last changes fastest.
Arguments:
- sym_press: float32 [4, 64, 8192], P('case', None, 'box'), parts along dimension 0, may hold values from -0.15625 to 0.15625
- anti_press: float32 [4, 64, 8192], P('case', None, 'box'), parts along dimension 0, may hold values from -0.15625 to 0.15625
- box_geom: float32 [3, 8192], P(None, 'box'), may hold values from 0.25 to 2
- box_station: int32 [8192], P('box'), may hold values from 0 to 31, as said below
- station_geom: float32 [2, 32], P(None, 'box'), may hold values from 0.25 to 2
- gust_index: int32 [64], replicated, may hold values from 0 to 255
Outputs:
- load_hist: bfloat16 [64, 3, 2, 64, 512], P(('case', 'box')), parts along dimension 0
There are 2 independent parts, one for each index of `case`. A program takes and returns all parts, laid end to end along the dimension named above; an argument that names none is the same for every part. Nothing has to cross between parts.
Inputs may be any that keep to these rules, and one draw needn't show every extreme that they name: `box_station`: station ids never fall along the boxes; the first box of station s lies in box block s // 2 (boxes d * 512 to (d + 1) * 512 - 1 hold the first boxes of stations d * 2 to (d + 1) * 2 - 1, and their other boxes belong to station d * 2 - 1; box 0 always opens station 0).
All inputs are finite; a program needn't handle non-finite values.
Results may differ from a plain program's by a relative error of at most 0.0086.
Values sent between devices are 32-bit elements; how exact they have to be, the bound alone decides.
No kernel may reach another device: no remote copies, remote signals or barrier semaphores. Data moves between devices by JAX's collectives and lax.ppermute only.
A program may use at most 64 MiB of HBM per device.

v0:
```python
import math

import jax
import jax.numpy as jnp
from jax import lax
from jax.sharding import PartitionSpec as P

NFFT = 512


def from_partner(block, axis, bit):
    count = lax.axis_size(axis)
    route = []
    for low in range(count):
        high = low | 1 << bit
        if high != low and high < count:
            route += [(low, high), (high, low)]
    return lax.ppermute(block, axis, route)


def angle_table(count_a, count_b, length):
    product = (
        jnp.arange(count_a, dtype=jnp.int32)[:, None]
        * jnp.arange(count_b, dtype=jnp.int32)[None, :]
        % length
    )
    return product.astype(jnp.float32) * (2.0 * math.pi / length)


def gust_spectrum(gust_index, freqs, length):
    steps = jnp.arange(length, dtype=jnp.int32)
    samples = gust_index + 8
    phase = steps.astype(jnp.float32)[None, :] / samples.astype(jnp.float32)[:, None]
    profile = jnp.where(
        steps[None, :] < samples[:, None], 0.5 - 0.5 * jnp.cos(2.0 * math.pi * phase), 0.0
    )
    theta = angle_table(length, freqs, length)
    spec_re = jnp.dot(profile, jnp.cos(theta), precision=lax.Precision.HIGHEST)
    spec_im = -jnp.dot(profile, jnp.sin(theta), precision=lax.Precision.HIGHEST)
    return (spec_re, spec_im)


def weighted(press, geom):
    area = geom[0]
    weights = jnp.stack([area, area * geom[1], area * geom[2]])
    return (press[:, None] * weights[None, :, None, None, :]).astype(jnp.bfloat16)


def station_loads(cut, station_geom):
    cut_y = station_geom[0][:, None, None]
    cut_x = station_geom[1][:, None, None]

    def arms(part):
        shear = part[:, 0]
        return jnp.stack([shear, part[:, 1] - cut_y * shear, part[:, 2] - cut_x * shear], 1)

    left_part = arms(cut[:, 0])
    right_part = arms(cut[:, 1])
    return jnp.stack([left_part + right_part, left_part - right_part], 2)


def histories(loads, spec_re, spec_im, length):
    freqs = loads.shape[-1]
    load_re = loads[..., 0, :][..., None, :]
    load_im = loads[..., 1, :][..., None, :]
    resp_re = spec_re * load_re - spec_im * load_im
    resp_im = spec_re * load_im + spec_im * load_re
    response = jnp.concatenate([resp_re, resp_im], -1).astype(jnp.bfloat16)
    phi = angle_table(freqs, length, length)
    factor = (jnp.where(jnp.arange(freqs) == 0, 1.0, 2.0) / length).astype(jnp.float32)[:, None]
    basis = jnp.concatenate([factor * jnp.cos(phi), -factor * jnp.sin(phi)], 0).astype(jnp.bfloat16)
    flat = jnp.dot(response.reshape(-1, 2 * freqs), basis, preferred_element_type=jnp.float32)
    return flat.astype(jnp.bfloat16).reshape(response.shape[:-1] + (length,))


def cut_mask(station_ids, count):
    column = lax.iota(jnp.int32, count)
    return (station_ids[:, None] >= column[None, :]).astype(jnp.bfloat16)


def on_device(sym_press, anti_press, box_geom, box_station, station_geom, gust_index):
    devices = lax.axis_size("box")
    half_bit = devices.bit_length() - 2
    freqs = sym_press.shape[1]
    box_dev = sym_press.shape[2]
    s_dev = station_geom.shape[1]
    stations = s_dev * devices
    rows_all = 12 * freqs
    anti_true = from_partner(anti_press, "box", half_bit)
    terms = weighted(jnp.stack([sym_press, anti_true]), box_geom).reshape(rows_all, box_dev)
    own_mask = cut_mask(box_station, stations)
    result = jnp.dot(terms, own_mask, preferred_element_type=jnp.float32)
    freq_major = lax.psum_scatter(result, "box", scatter_dimension=0, tiled=True)
    station_major = lax.all_to_all(freq_major, "box", split_axis=1, concat_axis=0, tiled=True)
    cut = station_major.T
    loads = station_loads(cut.reshape(s_dev, 2, 3, 2, freqs), station_geom)
    spec_re, spec_im = gust_spectrum(gust_index, freqs, NFFT)
    return histories(loads, spec_re, spec_im, NFFT)


def solution(mesh):
    placed = (
        P("case", None, "box"),
        P("case", None, "box"),
        P(None, "box"),
        P("box"),
        P(None, "box"),
        P(),
    )
    return jax.shard_map(
        on_device,
        mesh=mesh,
        in_specs=placed,
        out_specs=P(("case", "box"), None, None, None, None),
        check_vma=False,
    )
```

profile of v0, /device:TPU:0, one launch (start us, length us, event | category | flops | bytes accessed | tf_op | source)
XLA Modules:
  0.0 101.9 jit_solution(11784585565035401812)
XLA Ops:
  6.5 0.0 reduce-scatter.4.cloned.1.call-start
  6.5 4.0 %collective-permute-start = (f32[2,64,512]{2,1,0:T(8,128)}, f32[2,64,512]{2,1,0:T(8,128)S(1)}, u32[]{:S(2)}, u32[]{:S(2)}) collective-permute-start(f32[2,64,512]{2,1,0:T(8,128)} %param.7), channel_id=1, source_target_pairs={{0,8},{8,0},{1,9},{9,1},{2,10},{10,2},{3,11},{11,3},{4,12},{12,4},... | collective-permute-start | bytes 786440 | tf_op jit(solution)/shard_map/ppermute | solution.py:18
  10.6 0.8 fusion.71
  11.4 0.7 broadcast_add_fusion
  12.1 0.0 copy-start
  12.1 1.7 %convolution_negate_fusion = f32[64,64]{1,0:T(8,128)S(1)} fusion(f32[64]{0:T(128)S(1)} %get-tuple-element.25, f32[512]{0:T(512)S(1)} %iota_convert_fusion, s32[64]{0:T(128)S(1)} %get-tuple-element.24), kind=kOutput, calls=%fused_computation.2 | convolution fusion | flops 25825280 | bytes 18944 | tf_op jit(solution)/shard_map/dot_general | solution.py:39
  13.8 0.6 multiply_convert_fusion.1
  14.4 8.3 %collective-permute-done = f32[2,64,512]{2,1,0:T(8,128)S(1)} collective-permute-done((f32[2,64,512]{2,1,0:T(8,128)}, f32[2,64,512]{2,1,0:T(8,128)S(1)}, u32[]{:S(2)}, u32[]{:S(2)}) %collective-permute-start) | collective-permute-done | bytes 262176 | tf_op jit(solution)/shard_map/ppermute | solution.py:18
  22.7 0.0 copy-done
  22.7 0.0 copy-start.1
  22.8 0.1 multiply_convert_fusion
  22.9 0.5 copy-done.1
  23.4 1.2 %fusion.9 = f32[768,32]{1,0:T(8,128)} fusion(bf16[768,512]{1,0:T(8,128)(2,1)S(1)} %bitcast.56, s32[512]{0:T(512)S(1)} %copy-done.1), kind=kOutput, calls=%fused_computation.19 | convolution fusion | flops 25182208 | bytes 886784
  24.6 0.0 reduce-scatter.4.cloned.1.call-update
  24.7 0.0 copy-start.2
  24.7 1.7 %fusion.4 = f32[64,64]{1,0:T(8,128)S(1)} fusion(f32[64]{0:T(128)S(1)} %get-tuple-element.25, f32[512]{0:T(512)S(1)} %iota_convert_fusion, s32[64]{0:T(128)S(1)} %get-tuple-element.24), kind=kOutput, calls=%fused_computation.14 | convolution fusion | flops 25821184 | bytes 18944 | tf_op jit(solution)/shard_map/dot_general | solution.py:38
  26.4 55.2 %reduce-scatter.4.cloned.1.call-done = f32[48,32]{1,0:T(8,128)} async-done(((f32[768,32]{1,0:T(8,128)}), f32[48,32]{1,0:T(8,128)}) %reduce-scatter.4.cloned.1.call-update) | async-done | bytes 6160
  81.6 1.4 %copy.27 = f32[48,32]{0,1:T(8,128)} copy(f32[48,32]{1,0:T(8,128)} %reduce-scatter.4.cloned.1.call-done) | data formatting | bytes 12288
  83.0 3.7 %all-to-all-start = ((f32[48,16,2]{0,2,1:T(2,128)}), f32[48,16,2]{0,2,1:T(2,128)S(1)}, u32[]{:S(2)}, u32[]{:S(2)}) async-start(f32[48,16,2]{0,2,1:T(2,128)} %bitcast.3), calls=%async_computation | async-start | bytes 32768 | tf_op jit(solution)/shard_map/all_to_all | solution.py:94
  86.8 0.0 copy-done.2
  86.8 6.5 %all-to-all-done = f32[48,16,2]{0,2,1:T(2,128)S(1)} async-done(((f32[48,16,2]{0,2,1:T(2,128)}), f32[48,16,2]{0,2,1:T(2,128)S(1)}, u32[]{:S(2)}, u32[]{:S(2)}) %all-to-all-start) | async-done | bytes 6176 | tf_op jit(solution)/shard_map/all_to_all | solution.py:94
  93.3 0.1 all_to_all.17
  93.4 0.1 reshape.218
  93.5 0.1 slice_bitcast_fusion.2
  93.5 0.1 slice_bitcast_fusion.3
  93.7 0.1 subtract_convert_fusion
  93.8 1.3 %convolution_convert_fusion = bf16[768,512]{1,0:T(8,128)(2,1)} fusion(bf16[768,64]{1,0:T(8,128)(2,1)S(1)} %bitcast.58, bf16[768,64]{1,0:T(8,128)(2,1)S(1)} %bitcast.57, bf16[64,512]{1,0:T(8,128)(2,1)S(1)} %get-tuple-element.26, bf16[64,512]{1,0:T(8,128)(2,1)S(1)} %get-tuple-element.27), kind=kOutput, calls=%fused_computation.1 | convolution fusion | flops 101711872 | bytes 1114112 | tf_op jit(solution)/shard_map/dot_general | solution.py:72
  (13 shorter events, 0.1 us)
Async XLA Ops:
  6.5 75.1 %reduce-scatter.4.cloned.1.call-start = ((), (), s32[]{:S(2)}) async-start(), calls=%async_computation.2 | async-start | bytes 417792
  6.5 16.2 %collective-permute-start = (f32[2,64,512]{2,1,0:T(8,128)}, f32[2,64,512]{2,1,0:T(8,128)S(1)}, u32[]{:S(2)}, u32[]{:S(2)}) collective-permute-start(f32[2,64,512]{2,1,0:T(8,128)} %param.7), channel_id=1, source_target_pairs={{0,8},{8,0},{1,9},{9,1},{2,10},{10,2},{3,11},{11,3},{4,12},{12,4},... | collective-permute-start | bytes 786440 | tf_op jit(solution)/shard_map/ppermute | solution.py:18
  12.1 10.6 %copy-start = (f32[2,64,512]{2,1,0:T(8,128)S(1)}, f32[2,64,512]{2,1,0:T(8,128)}, u32[]{:S(2)}) copy-start(f32[2,64,512]{2,1,0:T(8,128)} %param.6) | copy-start | bytes 786436
  22.7 0.7 copy-start.1
  24.7 62.1 %copy-start.2 = (f32[2,2]{1,0:T(2,128)S(1)}, f32[2,2]{1,0:T(2,128)}, u32[]{:S(2)}) copy-start(f32[2,2]{1,0:T(2,128)} %param.10) | copy-start | bytes 52
  83.0 10.2 %all-to-all-start = ((f32[48,16,2]{0,2,1:T(2,128)}), f32[48,16,2]{0,2,1:T(2,128)S(1)}, u32[]{:S(2)}, u32[]{:S(2)}) async-start(f32[48,16,2]{0,2,1:T(2,128)} %bitcast.3), calls=%async_computation | async-start | bytes 32768 | tf_op jit(solution)/shard_map/all_to_all | solution.py:94
Sparse Core Ops, SparseCore 0:
  24.8 56.7 reduce-scatter.3
where the time goes:
time: 102 us
  waiting for transfers between devices  70.1 us (69%)
  between operations  13.5 us (13%)
  starting transfers between devices  7.76 us (8%)
  matrix products  5.93 us (6%)
  other arithmetic  2.5 us (2%)
  local copies, waits for them, and re-layouts  2.16 us (2%)
    unnamed x2, waiting for transfers between devices  55.2 us
    ppermute x1, waiting for transfers between devices, from_partner(): return lax.ppermute(block, axis, route)  8.34 us
    all_to_all x1, waiting for transfers between devices, on_device(): lax.all_to_all(freq_major, 'box', split_axis=1, concat_axis=0, tiled=True)  6.47 us
    ppermute x1, starting transfers between devices, from_partner(): return lax.ppermute(block, axis, route)  4.04 us
    all_to_all x1, starting transfers between devices, on_device(): lax.all_to_all(freq_major, 'box', split_axis=1, concat_axis=0, tiled=True)  3.73 us
  transfers between devices with their start and end apart: 3, of which 3 were waited for; matrix products, arithmetic and copies ran while one was open for 5% of the time, Pallas kernels for 0%

commit v1 on v0

v1 whole, which is shorter than its diff:
```python
import math

import jax
import jax.numpy as jnp
import numpy as np
from jax import lax
from jax.sharding import PartitionSpec as P

NFFT = 512
FIRST_GUST = 8


def swap(block, axis, mask):
    count = lax.axis_size(axis)
    return lax.ppermute(block, axis, [(i, i ^ mask) for i in range(count)])


def fourier_rows(freqs, length):
    turns = np.arange(freqs)[:, None] * np.arange(length)[None, :] % length
    angle = turns * (2.0 * math.pi / length)
    return np.concatenate([np.cos(angle), -np.sin(angle)]).astype(np.float32)


def gust_spectrum(gust_index, rows):
    steps = jnp.arange(rows.shape[1], dtype=jnp.int32)
    samples = gust_index + FIRST_GUST
    phase = steps.astype(jnp.float32)[None, :] / samples.astype(jnp.float32)[:, None]
    profile = jnp.where(steps[None, :] < samples[:, None], 0.5 - 0.5 * jnp.cos(2.0 * math.pi * phase), 0.0)
    return lax.dot_general(profile, rows, (((1,), (1,)), ((), ())), precision=lax.Precision.HIGHEST)


def block_sums(press, geom, first, s_dev):
    area = geom[0]
    weights = jnp.stack([area, area * geom[1], area * geom[2]])
    ids = geom[3]
    marks = first + jnp.arange(s_dev, dtype=jnp.int32)
    masks = jnp.concatenate([jnp.ones_like(ids)[None], (ids[None] >= marks.astype(jnp.float32)[:, None]).astype(jnp.float32)])
    rows = (masks[:, None] * weights[None]).reshape(-1, weights.shape[1])
    flat = press.reshape(-1, press.shape[-1])
    sums = lax.dot_general(rows, flat, (((1,), (1,)), ((), ())), precision=lax.Precision.HIGHEST)
    return sums.reshape(1 + s_dev, 3, -1)


def on_device(sym_press, anti_press, box_geom, box_station, station_geom, gust_index):
    devices = lax.axis_size("box")
    me = lax.axis_index("box")
    half = devices // 2
    freqs = sym_press.shape[1]
    s_dev = station_geom.shape[1]

    geom = jnp.concatenate([box_geom, box_station.astype(jnp.float32)[None]])
    partner_geom = swap(geom, "box", half)
    sym = block_sums(sym_press, geom, me * s_dev, s_dev)
    anti = block_sums(anti_press, partner_geom, (me ^ half) * s_dev, s_dev)

    def later(mask, flip):
        return (((me ^ mask ^ flip) > (me ^ flip)).astype(jnp.float32))

    total = jnp.stack([sym[0], anti[0]])
    sym_part = sym[1:]
    anti_part = anti[1:]
    bits = devices.bit_length() - 1
    digits = []
    low = 0
    while low < bits:
        size = 2 if low + 2 <= bits else 1
        digits.append((low, size))
        low += size
    for low, size in digits[:-1]:
        masks = [v << low for v in range(1, 1 << size)]
        got = [swap(total, "box", mask) for mask in masks]
        for mask, part in zip(masks, got):
            sym_part = sym_part + later(mask, 0) * part[0]
            anti_part = anti_part + later(mask, half) * part[1]
        total = total + sum(got)
    low, size = digits[-1]
    masks = [v << low for v in range(1, 1 << size)]
    own_total = total
    home = swap(jnp.concatenate([anti_part, total[:1]]), "box", half)
    others = {mask: swap(total, "box", mask) for mask in masks if mask != half}
    anti_part = home[:-1] + later(half, 0) * own_total[1]
    sym_part = sym_part + later(half, 0) * home[-1]
    for mask, part in others.items():
        sym_part = sym_part + later(mask, 0) * part[0]
        anti_part = anti_part + later(mask ^ half, 0) * part[1]

    arm = station_geom[:, :, None]

    def arms(part):
        return jnp.stack([part[:, 0], part[:, 1] - arm[0] * part[:, 0], part[:, 2] - arm[1] * part[:, 0]], 1)

    left, right = arms(sym_part), arms(anti_part)
    loads = jnp.stack([left + right, left - right], 2)[..., None, :]
    rows = fourier_rows(freqs, NFFT)
    spec = gust_spectrum(gust_index, jnp.asarray(rows))
    spec_re, spec_im = spec[:, :freqs], spec[:, freqs:]
    load_re, load_im = loads[..., :freqs], loads[..., freqs:]
    response = jnp.concatenate(
        [spec_re * load_re - spec_im * load_im, spec_re * load_im + spec_im * load_re], -1
    ).astype(jnp.bfloat16)
    scale = np.where(np.arange(2 * freqs) % freqs == 0, 1.0, 2.0)[:, None] / NFFT
    basis = jnp.asarray((rows * scale).astype(np.float32)).astype(jnp.bfloat16)
    flat = jnp.dot(response.reshape(-1, 2 * freqs), basis, preferred_element_type=jnp.float32)
    return flat.astype(jnp.bfloat16).reshape(response.shape[:-1] + (NFFT,))


def solution(mesh):
    placed = (
        P("case", None, "box"),
        P("case", None, "box"),
        P(None, "box"),
        P("box"),
        P(None, "box"),
        P(),
    )
    return jax.shard_map(
        on_device,
        mesh=mesh,
        in_specs=placed,
        out_specs=P(("case", "box"), None, None, None, None),
        check_vma=False,
    )
```

time: 102 us -> 22.9 us (0.22)
  waiting for transfers between devices: 70.1 us -> 4.14 us
  between operations: 13.5 us -> 0.26 us
  starting transfers between devices: 7.76 us -> 10.5 us
  matrix products: 5.93 us -> 3.92 us
  local copies, waits for them, and re-layouts: 2.16 us -> 0.24 us
  other arithmetic: 2.5 us -> 3.52 us
    unnamed x2 -> x0, waiting for transfers between devices: 55.2 us -> none
    all_to_all x1 -> x0, waiting for transfers between devices: 6.47 us -> none  [on_device(): lax.all_to_all(freq_major, 'box', split_axis=1, concat_axis=0, tiled=True)]
    ppermute x1 -> x7, starting transfers between devices: 4.04 us -> 10.5 us  [swap(): return lax.ppermute(block, axis, [(i, i ^ mask) for i in range(count)])]
    ppermute x1 -> x7, waiting for transfers between devices: 8.34 us -> 4.14 us  [swap(): return lax.ppermute(block, axis, [(i, i ^ mask) for i in range(count)])]
    all_to_all x1 -> x0, starting transfers between devices: 3.73 us -> none  [on_device(): lax.all_to_all(freq_major, 'box', split_axis=1, concat_axis=0, tiled=True)]
    unnamed x8 -> x10, local copies, waits for them, and re-layouts: 1.97 us -> 0.02 us
    unnamed x1 -> x0, matrix products: 1.22 us -> none
    dot_general x3 -> x5, matrix products: 4.71 us -> 3.92 us  [the longest x1 1.81 us: gust_spectrum(): lax.dot_general(profile, rows, (((1,), (1,)), ((), ())), precision=lax.Pr...]
  transfers between devices with their start and end apart: 3 -> 7, of which waited for: 3 -> 4; matrix products, arithmetic and copies ran while one was open for 5% -> 17% of each run, Pallas kernels for 0% -> 0%
where the time goes in v1:
time: 22.9 us; the launch traced here: 22.6 us
  starting transfers between devices  10.5 us (46%)
  waiting for transfers between devices  4.14 us (18%)
  matrix products  3.92 us (17%)
  other arithmetic  3.52 us (15%)
  between operations  0.26 us (1%)
  local copies, waits for them, and re-layouts  0.24 us (1%)
    ppermute x7, starting transfers between devices, swap(): return lax.ppermute(block, axis, [(i, i ^ mask) for i in range(count)])  10.5 us
    ppermute x7, waiting for transfers between devices, swap(): return lax.ppermute(block, axis, [(i, i ^ mask) for i in range(count)])  4.14 us
    dot_general x1, matrix products, gust_spectrum(): lax.dot_general(profile, rows, (((1,), (1,)), ((), ())), precision=lax.Pr...  1.81 us
    dot_general x2, matrix products, on_device(): jnp.dot(response.reshape(-1, 2 * freqs), basis, preferred_element_type=jn...  1.56 us
    slice x1, other arithmetic, block_sums(): area = geom[0]  0.81 us
    convert_element_type x1, other arithmetic, on_device(): geom = jnp.concatenate([box_geom, box_station.astype(jnp.float32)[None]])  0.75 us
    concatenate x1, other arithmetic, on_device(): geom = jnp.concatenate([box_geom, box_station.astype(jnp.float32)[None]])  0.7 us
    add x1, other arithmetic, gust_spectrum(): samples = gust_index + FIRST_GUST  0.66 us
  transfers between devices with their start and end apart: 7, of which 4 were waited for; matrix products, arithmetic and copies ran while one was open for 17% of the time, Pallas kernels for 0%

profile of v1, /device:TPU:0, one launch (start us, length us, event | category | flops | bytes accessed | tf_op | source)
XLA Modules:
  0.0 22.6 jit_solution(12697799288756511281)
XLA Ops:
  0.0 0.7 %convert_element_type.69 = f32[512]{0:T(512)S(1)} convert(s32[512]{0:T(512)} %param.11) | non-fusion elementwise | flops 512 | bytes 4096 | tf_op jit(solution)/shard_map/convert_element_type | solution.py:51
  0.8 0.7 %pad_maximum_fusion.1 = f32[4,512]{1,0:T(4,128)S(1)} fusion(f32[1,512]{1,0:T(1,128)S(1)} %bitcast.72, f32[3,512]{1,0:T(4,128)} %param.10), kind=kLoop, calls=%fused_computation.19 | loop fusion | flops 2048 | bytes 16384 | tf_op jit(solution)/shard_map/concatenate | solution.py:51
  1.5 4.0 %collective-permute-start = (f32[4,512]{1,0:T(4,128)S(1)}, f32[4,512]{1,0:T(4,128)S(1)}, u32[]{:S(2)}, u32[]{:S(2)}) collective-permute-start(f32[4,512]{1,0:T(4,128)S(1)} %pad_maximum_fusion.1), channel_id=1, source_target_pairs={{0,8},{1,9},{2,10},{3,11},{4,12},{5,13},{6,14},{7,15},{8,0},{9,1},... | collective-permute-start | bytes 24584 | tf_op jit(solution)/shard_map/ppermute | solution.py:15
  5.5 0.8 %fusion.38 = (f32[1,512]{1,0:T(1,128)S(1)}, f32[1,512]{1,0:T(1,128)S(1)}, f32[1,512]{1,0:T(1,128)S(1)}) fusion(f32[3,512]{1,0:T(4,128)} %param.10), kind=kLoop, calls=%fused_computation.93 | loop fusion | flops 1024 | bytes 12288 | tf_op jit(solution)/shard_map/slice | solution.py:33
  6.3 0.7 %broadcast_add_fusion = (s32[64]{0:T(128)S(1)}, f32[64]{0:T(128)S(1)}) fusion(s32[64]{0:T(128)} %param.13), kind=kLoop, calls=%fused_computation.85 | loop fusion | flops 128 | bytes 768 | tf_op jit(solution)/shard_map/add | solution.py:26
  7.0 0.1 broadcast_compare_fusion.1
  7.1 1.8 %fusion.4 = f32[64,128]{1,0:T(8,128)S(1)} fusion(f32[128,512]{1,0:T(8,128)} %constant.30.clone, f32[64]{0:T(128)S(1)} %get-tuple-element.44, f32[512]{0:T(512)S(1)} %iota_convert_fusion, s32[64]{0:T(128)S(1)} %get-tuple-element.43), kind=kOutput, calls=%fused_computation.9 | convolution fusion | flops 50528256 | bytes 297472 | tf_op jit(solution)/shard_map/dot_general | solution.py:29
  8.9 0.1 fusion.37
  9.0 0.3 %fusion.41 = f32[9,128]{1,0:T(8,128)S(1)} fusion(f32[9,512]{1,0:T(8,128)S(1)} %mul.257, f32[128,512]{1,0:T(8,128)S(1)} %bitcast.68), kind=kOutput, calls=%fused_computation.96 | convolution fusion | flops 7077888 | bytes 285184 | tf_op jit(solution)/shard_map/dot_general | solution.py:40
  9.3 0.1 add_convert_fusion.2
  9.4 0.0 collective-permute-done
  9.4 0.1 broadcast_compare_fusion
  9.5 0.3 %fusion.42 = f32[9,128]{1,0:T(8,128)S(1)} fusion(f32[9,512]{1,0:T(8,128)S(1)} %mul.265, f32[128,512]{1,0:T(8,128)S(1)} %bitcast.71), kind=kOutput, calls=%fused_computation.97 | convolution fusion | flops 7077888 | bytes 285184 | tf_op jit(solution)/shard_map/dot_general | solution.py:40
  9.8 0.1 pad_maximum_fusion.4
  9.9 0.7 %collective-permute-start.3 = (f32[2,3,128]{2,1,0:T(4,128)S(1)}, f32[2,3,128]{2,1,0:T(4,128)S(1)}, u32[]{:S(2)}, u32[]{:S(2)}) collective-permute-start(f32[2,3,128]{2,1,0:T(4,128)S(1)} %pad_maximum_fusion.4), channel_id=1, source_target_pairs={{0,3},{1,2},{2,1},{3,0},{4,7},{5,6},{6,5},{7,4},{8,11},{9,10},{10,... | collective-permute-start | bytes 9224 | tf_op jit(solution)/shard_map/ppermute | solution.py:15
  10.6 0.9 %collective-permute-start.2 = (f32[2,3,128]{2,1,0:T(4,128)S(1)}, f32[2,3,128]{2,1,0:T(4,128)S(1)}, u32[]{:S(2)}, u32[]{:S(2)}) collective-permute-start(f32[2,3,128]{2,1,0:T(4,128)S(1)} %pad_maximum_fusion.4), channel_id=1, source_target_pairs={{0,2},{1,3},{2,0},{3,1},{4,6},{5,7},{6,4},{7,5},{8,10},{9,11},{10,... | collective-permute-start | bytes 9224 | tf_op jit(solution)/shard_map/ppermute | solution.py:15
  11.5 0.3 %collective-permute-start.1 = (f32[2,3,128]{2,1,0:T(4,128)S(1)}, f32[2,3,128]{2,1,0:T(4,128)S(1)}, u32[]{:S(2)}, u32[]{:S(2)}) collective-permute-start(f32[2,3,128]{2,1,0:T(4,128)S(1)} %pad_maximum_fusion.4), channel_id=1, source_target_pairs={{0,1},{1,0},{2,3},{3,2},{4,5},{5,4},{6,7},{7,6},{8,9},{9,8},{10,11... | collective-permute-start | bytes 9224 | tf_op jit(solution)/shard_map/ppermute | solution.py:15
  11.9 1.1 %collective-permute-done.3 = f32[2,3,128]{2,1,0:T(4,128)S(1)} collective-permute-done((f32[2,3,128]{2,1,0:T(4,128)S(1)}, f32[2,3,128]{2,1,0:T(4,128)S(1)}, u32[]{:S(2)}, u32[]{:S(2)}) %collective-permute-start.3) | collective-permute-done | bytes 3104 | tf_op jit(solution)/shard_map/ppermute | solution.py:15
  13.0 1.3 %collective-permute-done.2 = f32[2,3,128]{2,1,0:T(4,128)S(1)} collective-permute-done((f32[2,3,128]{2,1,0:T(4,128)S(1)}, f32[2,3,128]{2,1,0:T(4,128)S(1)}, u32[]{:S(2)}, u32[]{:S(2)}) %collective-permute-start.2) | collective-permute-done | bytes 3104 | tf_op jit(solution)/shard_map/ppermute | solution.py:15
  14.3 0.0 collective-permute-done.1
  14.3 1.4 %collective-permute-start.6 = (f32[2,3,128]{2,1,0:T(4,128)S(1)}, f32[2,3,128]{2,1,0:T(4,128)S(1)}, u32[]{:S(2)}, u32[]{:S(2)}) collective-permute-start(f32[2,3,128]{2,1,0:T(4,128)S(1)} %add_add_fusion), channel_id=1, source_target_pairs={{0,12},{1,13},{2,14},{3,15},{4,8},{5,9},{6,10},{7,11},{8,4},{9,5},... | collective-permute-start | bytes 9224 | tf_op jit(solution)/shard_map/ppermute | solution.py:15
  15.7 0.3 %collective-permute-start.5 = (f32[2,3,128]{2,1,0:T(4,128)S(1)}, f32[2,3,128]{2,1,0:T(4,128)S(1)}, u32[]{:S(2)}, u32[]{:S(2)}) collective-permute-start(f32[2,3,128]{2,1,0:T(4,128)S(1)} %add_add_fusion), channel_id=1, source_target_pairs={{0,4},{1,5},{2,6},{3,7},{4,0},{5,1},{6,2},{7,3},{8,12},{9,13},{10,... | collective-permute-start | bytes 9224 | tf_op jit(solution)/shard_map/ppermute | solution.py:15
  16.0 2.8 %collective-permute-start.4 = (f32[3,3,128]{2,1,0:T(4,128)S(1)}, f32[3,3,128]{2,1,0:T(4,128)S(1)}, u32[]{:S(2)}, u32[]{:S(2)}) collective-permute-start(f32[3,3,128]{2,1,0:T(4,128)S(1)} %pad_maximum_fusion.3), channel_id=1, source_target_pairs={{0,8},{1,9},{2,10},{3,11},{4,12},{5,13},{6,14},{7,15},{8,0},{9,1},... | collective-permute-start | bytes 13832 | tf_op jit(solution)/shard_map/ppermute | solution.py:15
  18.8 0.9 %collective-permute-done.6 = f32[2,3,128]{2,1,0:T(4,128)S(1)} collective-permute-done((f32[2,3,128]{2,1,0:T(4,128)S(1)}, f32[2,3,128]{2,1,0:T(4,128)S(1)}, u32[]{:S(2)}, u32[]{:S(2)}) %collective-permute-start.6) | collective-permute-done | bytes 3104 | tf_op jit(solution)/shard_map/ppermute | solution.py:15
  19.8 0.0 collective-permute-done.5
  19.8 0.9 %collective-permute-done.4 = f32[3,3,128]{2,1,0:T(4,128)S(1)} collective-permute-done((f32[3,3,128]{2,1,0:T(4,128)S(1)}, f32[3,3,128]{2,1,0:T(4,128)S(1)}, u32[]{:S(2)}, u32[]{:S(2)}) %collective-permute-start.4) | collective-permute-done | bytes 4640 | tf_op jit(solution)/shard_map/ppermute | solution.py:15
  20.7 0.1 slice_bitcast_fusion.4
  20.8 0.1 slice_bitcast_fusion.1
  20.9 0.1 add_convert_fusion.1
  21.0 0.3 %fusion.43 = f32[768,512]{1,0:T(8,128)S(1)} fusion(bf16[768,64]{1,0:T(8,128)(2,1)S(1)} %bitcast.70, bf16[64,512]{1,0:T(8,128)(2,1)S(1)} %copy-done.3), kind=kOutput, calls=%fused_computation.98 | convolution fusion | flops 50331648 | bytes 1736704 | tf_op jit(solution)/shard_map/dot_general | solution.py:103
  21.3 0.0 copy-done.2
  21.3 1.2 %add_convert_fusion = bf16[768,512]{1,0:T(8,128)(2,1)} fusion(f32[768,512]{1,0:T(8,128)S(1)} %fusion.43, bf16[768,64]{1,0:T(8,128)(2,1)S(1)} %bitcast.69, bf16[64,512]{1,0:T(8,128)(2,1)S(1)} %copy-done.2), kind=kOutput, calls=%fused_computation | convolution fusion | flops 51118080 | bytes 2523136 | tf_op jit(solution)/shard_map/dot_general | solution.py:103
  (44 shorter events, 0.2 us)
Async XLA Ops:
  0.0 9.0 %copy-start = (f32[2,64,512]{2,1,0:T(8,128)S(1)}, f32[2,64,512]{2,1,0:T(8,128)}, u32[]{:S(2)}) copy-start(f32[2,64,512]{2,1,0:T(8,128)} %param.8) | copy-start | bytes 786436
  0.0 21.0 %copy-start.3 = (bf16[64,512]{1,0:T(8,128)(2,1)S(1)}, bf16[64,512]{1,0:T(8,128)(2,1)}, u32[]{:S(2)}) copy-start(bf16[64,512]{1,0:T(8,128)(2,1)} %constant.38) | copy-start | bytes 196612
  0.0 9.5 %copy-start.1 = (f32[2,64,512]{2,1,0:T(8,128)S(1)}, f32[2,64,512]{2,1,0:T(8,128)}, u32[]{:S(2)}) copy-start(f32[2,64,512]{2,1,0:T(8,128)} %param.9) | copy-start | bytes 786436
  0.0 11.8 %copy-start.4 = (f32[2,2]{1,0:T(2,128)S(1)}, f32[2,2]{1,0:T(2,128)}, u32[]{:S(2)}) copy-start(f32[2,2]{1,0:T(2,128)} %param.12) | copy-start | bytes 52
  1.5 7.9 %collective-permute-start = (f32[4,512]{1,0:T(4,128)S(1)}, f32[4,512]{1,0:T(4,128)S(1)}, u32[]{:S(2)}, u32[]{:S(2)}) collective-permute-start(f32[4,512]{1,0:T(4,128)S(1)} %pad_maximum_fusion.1), channel_id=1, source_target_pairs={{0,8},{1,9},{2,10},{3,11},{4,12},{5,13},{6,14},{7,15},{8,0},{9,1},... | collective-permute-start | bytes 24584 | tf_op jit(solution)/shard_map/ppermute | solution.py:15
  9.5 11.9 %copy-start.2 = (bf16[64,512]{1,0:T(8,128)(2,1)S(1)}, bf16[64,512]{1,0:T(8,128)(2,1)}, u32[]{:S(2)}) copy-start(bf16[64,512]{1,0:T(8,128)(2,1)} %constant.39) | copy-start | bytes 196612
  9.9 3.1 %collective-permute-start.3 = (f32[2,3,128]{2,1,0:T(4,128)S(1)}, f32[2,3,128]{2,1,0:T(4,128)S(1)}, u32[]{:S(2)}, u32[]{:S(2)}) collective-permute-start(f32[2,3,128]{2,1,0:T(4,128)S(1)} %pad_maximum_fusion.4), channel_id=1, source_target_pairs={{0,3},{1,2},{2,1},{3,0},{4,7},{5,6},{6,5},{7,4},{8,11},{9,10},{10,... | collective-permute-start | bytes 9224 | tf_op jit(solution)/shard_map/ppermute | solution.py:15
  10.6 3.6 %collective-permute-start.2 = (f32[2,3,128]{2,1,0:T(4,128)S(1)}, f32[2,3,128]{2,1,0:T(4,128)S(1)}, u32[]{:S(2)}, u32[]{:S(2)}) collective-permute-start(f32[2,3,128]{2,1,0:T(4,128)S(1)} %pad_maximum_fusion.4), channel_id=1, source_target_pairs={{0,2},{1,3},{2,0},{3,1},{4,6},{5,7},{6,4},{7,5},{8,10},{9,11},{10,... | collective-permute-start | bytes 9224 | tf_op jit(solution)/shard_map/ppermute | solution.py:15
  11.5 2.7 %collective-permute-start.1 = (f32[2,3,128]{2,1,0:T(4,128)S(1)}, f32[2,3,128]{2,1,0:T(4,128)S(1)}, u32[]{:S(2)}, u32[]{:S(2)}) collective-permute-start(f32[2,3,128]{2,1,0:T(4,128)S(1)} %pad_maximum_fusion.4), channel_id=1, source_target_pairs={{0,1},{1,0},{2,3},{3,2},{4,5},{5,4},{6,7},{7,6},{8,9},{9,8},{10,11... | collective-permute-start | bytes 9224 | tf_op jit(solution)/shard_map/ppermute | solution.py:15
  14.3 5.5 %collective-permute-start.6 = (f32[2,3,128]{2,1,0:T(4,128)S(1)}, f32[2,3,128]{2,1,0:T(4,128)S(1)}, u32[]{:S(2)}, u32[]{:S(2)}) collective-permute-start(f32[2,3,128]{2,1,0:T(4,128)S(1)} %add_add_fusion), channel_id=1, source_target_pairs={{0,12},{1,13},{2,14},{3,15},{4,8},{5,9},{6,10},{7,11},{8,4},{9,5},... | collective-permute-start | bytes 9224 | tf_op jit(solution)/shard_map/ppermute | solution.py:15
  15.7 4.1 %collective-permute-start.5 = (f32[2,3,128]{2,1,0:T(4,128)S(1)}, f32[2,3,128]{2,1,0:T(4,128)S(1)}, u32[]{:S(2)}, u32[]{:S(2)}) collective-permute-start(f32[2,3,128]{2,1,0:T(4,128)S(1)} %add_add_fusion), channel_id=1, source_target_pairs={{0,4},{1,5},{2,6},{3,7},{4,0},{5,1},{6,2},{7,3},{8,12},{9,13},{10,... | collective-permute-start | bytes 9224 | tf_op jit(solution)/shard_map/ppermute | solution.py:15
  16.0 4.6 %collective-permute-start.4 = (f32[3,3,128]{2,1,0:T(4,128)S(1)}, f32[3,3,128]{2,1,0:T(4,128)S(1)}, u32[]{:S(2)}, u32[]{:S(2)}) collective-permute-start(f32[3,3,128]{2,1,0:T(4,128)S(1)} %pad_maximum_fusion.3), channel_id=1, source_target_pairs={{0,8},{1,9},{2,10},{3,11},{4,12},{5,13},{6,14},{7,15},{8,0},{9,1},... | collective-permute-start | bytes 13832 | tf_op jit(solution)/shard_map/ppermute | solution.py:15

commit v2 on v1

v2 whole, which is shorter than its diff:
```python
import math

import jax
import jax.numpy as jnp
import numpy as np
from jax import lax
from jax.experimental import pallas as pl
from jax.experimental.pallas import tpu as pltpu
from jax.sharding import PartitionSpec as P

NFFT = 512
FIRST_GUST = 8
LANES = 128


def swap(block, axis, mask):
    count = lax.axis_size(axis)
    return lax.ppermute(block, axis, [(i, i ^ mask) for i in range(count)])


def in_vmem(array):
    return pltpu.with_memory_space_constraint(array, pltpu.VMEM)


def fourier_rows(freqs, length):
    turns = np.arange(freqs)[:, None] * np.arange(length)[None, :] % length
    angle = turns * (2.0 * math.pi / length)
    return np.concatenate([np.cos(angle), -np.sin(angle)]).astype(np.float32)


def block_sums(press, geom, marks):
    area = geom[0:1]
    out = []
    for moment in range(3):
        weight = area if moment == 0 else area * geom[moment : moment + 1]
        terms = (press * weight).astype(jnp.bfloat16)
        out.append(
            lax.dot_general(marks, terms, (((1,), (1,)), ((), ())), preferred_element_type=jnp.float32)
        )
    return out


def station_marks(ids, s_dev):
    row = ids
    step = lax.broadcasted_iota(jnp.int32, (8, row.shape[1]), 0).astype(jnp.float32)
    last = row[:, row.shape[1] - 1 :]
    passed = jnp.broadcast_to(row - last, step.shape) >= step - s_dev
    return jnp.where((step == 0) | passed, 1.0, 0.0).astype(jnp.bfloat16)


def pack_kernel(geom_ref, ids_ref, out_ref):
    ids = ids_ref[...].astype(jnp.float32)
    out_ref[0:3] = geom_ref[...]
    out_ref[3:4] = jnp.concatenate([ids[i : i + 1] for i in range(ids.shape[0])], 1)


def pack_kernel(geom_ref, ids_ref, out_ref):
    ids = ids_ref[...].astype(jnp.float32)
    out_ref[0:3] = geom_ref[...]
    out_ref[3:4] = jnp.concatenate([ids[i : i + 1] for i in range(ids.shape[0])], 1)


def sym_kernel(s_dev, sym_ref, anti_ref, geom_ref, total_ref, part_ref, held_ref):
    rows = held_ref.shape[0]
    held_ref[...] = anti_ref[...].reshape(held_ref.shape)
    geom = geom_ref[...]
    sums = block_sums(sym_ref[...].reshape(rows, -1), geom, station_marks(geom[3:4], s_dev))
    for moment in range(3):
        total_ref[moment : moment + 1] = sums[moment][0:1]
        for k in range(s_dev):
            part_ref[k, moment : moment + 1] = sums[moment][1 + k : 2 + k]


def anti_kernel(s_dev, geom_ref, held_ref, total_ref, part_ref):
    geom = geom_ref[...]
    sums = block_sums(held_ref[...], geom, station_marks(geom[3:4], s_dev))
    for moment in range(3):
        total_ref[moment : moment + 1] = sums[moment][0:1]
        for k in range(s_dev):
            part_ref[k, moment : moment + 1] = sums[moment][1 + k : 2 + k]


def spectrum_kernel(index_ref, rows_ref, arm_ref, after_ref, spec_ref, arms_ref):
    for row in range(2):
        for s in range(arms_ref.shape[1]):
            arms_ref[row, s : s + 1] = jnp.broadcast_to(arm_ref[row : row + 1, s : s + 1], (1, arms_ref.shape[2]))
    gusts, length = spec_ref.shape[0], rows_ref.shape[1]
    index = jnp.broadcast_to(index_ref[...], (gusts, gusts))
    diagonal = lax.broadcasted_iota(jnp.int32, (gusts, gusts), 0) == lax.broadcasted_iota(
        jnp.int32, (gusts, gusts), 1
    )
    samples = jnp.sum(jnp.where(diagonal, index, 0), 1, keepdims=True) + FIRST_GUST
    steps = lax.broadcasted_iota(jnp.int32, (gusts, length), 1)
    phase = steps.astype(jnp.float32) / samples.astype(jnp.float32)
    profile = jnp.where(steps < samples, 0.5 - 0.5 * jnp.cos(2.0 * math.pi * phase), 0.0)
    spec_ref[...] = lax.dot_general(
        profile, rows_ref[...], (((1,), (1,)), ((), ())),
        precision=lax.Precision.HIGHEST, preferred_element_type=jnp.float32,
    )


def history_kernel(sym_ref, anti_ref, arm_ref, spec_ref, basis_ref, out_ref, rows_ref, sems):
    gusts, wide = spec_ref.shape
    freqs = wide // 2
    s_dev = sym_ref.shape[0]
    spec = spec_ref[...]
    lane = lax.broadcasted_iota(jnp.int32, (1, wide), 1)
    crossed = jnp.where(lane < freqs, -1.0, 1.0) * pltpu.roll(spec, freqs, 1)

    def arms(ref, s):
        shear = ref[s, 0:1]
        return [
            shear,
            ref[s, 1:2] - arm_ref[0, s : s + 1] * shear,
            ref[s, 2:3] - arm_ref[1, s : s + 1] * shear,
        ]

    copies = []
    for s in range(s_dev):
        left, right = arms(sym_ref, s), arms(anti_ref, s)
        for comp in range(3):
            blocks = []
            for load in (left[comp] + right[comp], left[comp] - right[comp]):
                turned = pltpu.roll(load, freqs, 1)
                load_re = jnp.where(lane < freqs, load, turned)
                load_im = jnp.where(lane < freqs, turned, load)
                blocks.append((spec * load_re + crossed * load_im).astype(jnp.bfloat16))
            first = (s * 3 + comp) * 2 * gusts
            here = pl.ds(first, 2 * gusts)
            rows_ref[here] = jnp.dot(
                jnp.concatenate(blocks), basis_ref[...], preferred_element_type=jnp.float32
            ).astype(jnp.bfloat16)
            copy = pltpu.make_async_copy(rows_ref.at[here], out_ref.at[here], sems.at[s * 3 + comp])
            copy.start()
            copies.append(copy)
    for copy in copies:
        copy.wait()


def on_device(sym_press, anti_press, box_geom, box_station, station_geom, gust_index):
    devices = lax.axis_size("box")
    me = lax.axis_index("box")
    half = devices // 2
    freqs = sym_press.shape[1]
    box_dev = sym_press.shape[2]
    s_dev = station_geom.shape[1]
    gusts = gust_index.shape[0]
    wide = 2 * freqs
    f32 = jnp.float32

    ids = box_station.reshape(-1, LANES)
    geom = pl.pallas_call(pack_kernel, out_shape=pltpu.VMEM((4, box_dev), f32), name="pack")(box_geom, ids)
    partner_geom = swap(geom, "box", half)
    sym_total, sym_part, held = pl.pallas_call(
        lambda *refs: sym_kernel(s_dev, *refs),
        out_shape=(
            pltpu.VMEM((3, wide), f32),
            pltpu.VMEM((s_dev, 3, wide), f32),
            pltpu.VMEM((wide, box_dev), f32),
        ),
        name="sym_sums",
    )(sym_press, anti_press, in_vmem(geom))
    anti_total, anti_part = pl.pallas_call(
        lambda *refs: anti_kernel(s_dev, *refs), out_shape=(pltpu.VMEM((3, wide), f32),pltpu.VMEM((s_dev, 3, wide), f32)), name="anti_sums"
    )(in_vmem(partner_geom), in_vmem(held))

    rows = fourier_rows(freqs, NFFT)
    spec, arm = pl.pallas_call(
        spectrum_kernel, out_shape=(pltpu.VMEM((gusts, wide), f32), pltpu.VMEM((2, s_dev, wide), f32)), name="spectrum"
    )(gust_index.reshape(1, gusts), in_vmem(jnp.asarray(rows)), station_geom, in_vmem(anti_total))
    scale = np.where(np.arange(wide) % freqs == 0, 1.0, 2.0)[:, None] / NFFT
    basis = jnp.asarray((rows * scale).astype(np.float32).astype(jnp.bfloat16))


    sent = jnp.concatenate([jnp.stack([sym_total, anti_total]), anti_part])
    got = swap(sent, "box", half ^ 1)
    is_low = (me < half).astype(f32)
    past = jnp.stack([got[0], anti_total]) * is_low
    total = jnp.stack([sym_total, got[1]])
    past, spec, arm = lax.optimization_barrier((past, spec, arm))
    state = jnp.concatenate([past, total])

    def later(mask):
        return ((me ^ mask) > me).astype(f32)

    got = swap(jnp.concatenate([state, got[2:]]), "box", 1)
    sym_part = sym_part + later(1) * got[2]
    anti_part = got[4:] + later(1) * total[1]
    state = state + got[:4]
    low, high = 1, half.bit_length() - 1
    while low < high:
        size = min(2, high - low)
        masks = [v << low for v in range(1, 1 << size)]
        parts = [swap(state, "box", mask ^ 1) for mask in masks]
        for mask, part in zip(masks, parts):
            sym_part = sym_part + later(mask) * part[2]
            anti_part = anti_part + later(mask) * part[3]
        state = state + sum(parts)
        low += size
    sym_part = sym_part + state[0]
    anti_part = anti_part + state[1]

    out = pl.pallas_call(
        history_kernel,
        out_shape=jax.ShapeDtypeStruct((s_dev * 6 * gusts, NFFT), jnp.bfloat16),
        out_specs=pl.BlockSpec(memory_space=pl.ANY),
        scratch_shapes=[
            pltpu.VMEM((s_dev * 6 * gusts, NFFT), jnp.bfloat16),
            pltpu.SemaphoreType.DMA((s_dev * 3,)),
        ],
        name="histories",
    )(in_vmem(sym_part), in_vmem(anti_part), in_vmem(arm), in_vmem(spec), in_vmem(basis))
    return out.reshape(s_dev, 3, 2, gusts, NFFT)


def solution(mesh):
    placed = (
        P("case", None, "box"),
        P("case", None, "box"),
        P(None, "box"),
        P("box"),
        P(None, "box"),
        P(),
    )
    return jax.shard_map(
        on_device,
        mesh=mesh,
        in_specs=placed,
        out_specs=P(("case", "box"), None, None, None, None),
        check_vma=False,
    )
```

time: 22.9 us -> 19.6 us (0.86)
  Pallas kernels: 0 us -> 4.99 us
  matrix products: 3.92 us -> 0 us
  other arithmetic: 3.52 us -> 0.08 us
  starting transfers between devices: 10.5 us -> 9.22 us
  waiting for transfers between devices: 4.14 us -> 4.95 us
    pallas_call x0 -> x5, Pallas kernels: none -> 4.99 us  [the longest x1 1.58 us: on_device(): pl.pallas_call(spectrum_kernel, out_shape=(pltpu.VMEM((gusts, wide), f32)...]
    dot_general x5 -> x0, matrix products: 3.92 us -> none  [the longest x1 1.81 us: gust_spectrum(): lax.dot_general(profile, rows, (((1,), (1,)), ((), ())), precision=lax.Pr...]
    ppermute x7 -> x6, starting transfers between devices: 10.5 us -> 9.22 us  [swap(): return lax.ppermute(block, axis, [(i, i ^ mask) for i in range(count)])]
    slice x2 -> x0, other arithmetic: 0.82 us -> none  [the longest x1 0.81 us: block_sums(): area = geom[0]]
    convert_element_type x4 -> x0, other arithmetic: 0.81 us -> none  [the longest x1 0.75 us: on_device(): geom = jnp.concatenate([box_geom, box_station.astype(jnp.float32)[None]])]
    ppermute x7 -> x6, waiting for transfers between devices: 4.14 us -> 4.95 us  [swap(): return lax.ppermute(block, axis, [(i, i ^ mask) for i in range(count)])]
    concatenate x4 -> x2, other arithmetic: 0.73 us -> 0.02 us  [the longest x1 0.01 us: on_device(): got = swap(jnp.concatenate([state, got[2:]]), 'box', 1)]
    add x13 -> x8, other arithmetic: 0.72 us -> 0.05 us  [the longest x3 0.02 us: on_device(): anti_part = anti_part + later(mask) * part[3]]
  transfers between devices with their start and end apart: 7 -> 6, of which waited for: 4 -> 6; matrix products, arithmetic and copies ran while one was open for 17% -> 0% of each run, Pallas kernels for 0% -> 15%
where the time goes in v2:
time: 19.6 us; the launch traced here: 19.3 us
  starting transfers between devices  9.22 us (47%)
  Pallas kernels  4.99 us (25%)
  waiting for transfers between devices  4.95 us (25%)
    ppermute x6, starting transfers between devices, swap(): return lax.ppermute(block, axis, [(i, i ^ mask) for i in range(count)])  9.22 us
    ppermute x6, waiting for transfers between devices, swap(): return lax.ppermute(block, axis, [(i, i ^ mask) for i in range(count)])  4.95 us
    pallas_call x1, Pallas kernels, on_device(): pl.pallas_call(spectrum_kernel, out_shape=(pltpu.VMEM((gusts, wide), f32)...  1.58 us
    pallas_call x1, Pallas kernels, on_device(): pl.pallas_call(lambda *refs: sym_kernel(s_dev, *refs), out_shape=(pltpu.V...  1.29 us
    pallas_call x1, Pallas kernels, on_device(): pl.pallas_call(history_kernel, out_shape=jax.ShapeDtypeStruct((s_dev * 6...  1.17 us
    pallas_call x1, Pallas kernels, on_device(): pl.pallas_call(pack_kernel, out_shape=pltpu.VMEM((4, box_dev), f32), name...  0.71 us
  transfers between devices with their start and end apart: 6, of which 6 were waited for; matrix products, arithmetic and copies ran while one was open for 0% of the time, Pallas kernels for 15%

profile of v2, /device:TPU:0, one launch (start us, length us, event | category | flops | bytes accessed | tf_op | source)
XLA Modules:
  0.0 19.3 jit_solution(16606254529327045002)
XLA Ops:
  0.0 0.7 %pack.1.refs_2_ = f32[4,512]{1,0:T(4,128)S(1)} custom-call(f32[3,512]{1,0:T(4,128)} %geom_ref.1, s32[4,128]{1,0:T(4,128)} %bitcast.30), custom_call_target="tpu_custom_call" | custom-call | tf_op jit(solution)/shard_map/pack/pallas_call | solution.py:152
  0.7 4.0 %collective-permute-start = (f32[4,512]{1,0:T(4,128)S(1)}, f32[4,512]{1,0:T(4,128)S(1)}, u32[]{:S(2)}, u32[]{:S(2)}) collective-permute-start(f32[4,512]{1,0:T(4,128)S(1)} %pack.1.refs_2_), channel_id=1, source_target_pairs={{0,8},{1,9},{2,10},{3,11},{4,12},{5,13},{6,14},{7,15},{8,0},{9,1},... | collective-permute-start | bytes 24584 | tf_op jit(solution)/shard_map/ppermute | solution.py:18
  4.7 1.3 %sym_sums.1 = (f32[3,128]{1,0:T(4,128)S(1)}, f32[2,3,128]{2,1,0:T(4,128)S(1)}, f32[128,512]{1,0:T(8,128)S(1)}) custom-call(f32[2,64,512]{2,1,0:T(8,128)} %refs_0_.1, f32[2,64,512]{2,1,0:T(8,128)} %refs_1_.1, f32[4,512]{1,0:T(4,128)S(1)} %pack.1.refs_2_), custom_call_target="tpu_custom_call" | custom-call | tf_op jit(solution)/shard_map/sym_sums/pallas_call | solution.py:154
  6.0 0.0 copy-start
  6.0 0.3 %collective-permute-done.refs_0_ = f32[4,512]{1,0:T(4,128)S(1)} collective-permute-done((f32[4,512]{1,0:T(4,128)S(1)}, f32[4,512]{1,0:T(4,128)S(1)}, u32[]{:S(2)}, u32[]{:S(2)}) %collective-permute-start) | collective-permute-done | bytes 8224 | tf_op jit(solution)/shard_map/ppermute | solution.py:18
  6.4 0.2 %anti_sums.1 = (f32[3,128]{1,0:T(4,128)S(1)}, f32[2,3,128]{2,1,0:T(4,128)S(1)}) custom-call(f32[4,512]{1,0:T(4,128)S(1)} %collective-permute-done.refs_0_, f32[128,512]{1,0:T(8,128)S(1)} %get-tuple-element.17.refs_1_), custom_call_target="tpu_custom_call" | custom-call | tf_op jit(solution)/shard_map/anti_sums/pallas_call | solution.py:163
  6.6 1.3 %collective-permute-start.1 = (f32[4,3,128]{2,1,0:T(4,128)S(1)}, f32[4,3,128]{2,1,0:T(4,128)S(1)}, u32[]{:S(2)}, u32[]{:S(2)}) collective-permute-start(f32[4,3,128]{2,1,0:T(4,128)S(1)} %pad_maximum_fusion.1), channel_id=1, source_target_pairs={{0,9},{1,8},{2,11},{3,10},{4,13},{5,12},{6,15},{7,14},{8,1},{9,0},... | collective-permute-start | bytes 18440 | tf_op jit(solution)/shard_map/ppermute | solution.py:18
  7.9 0.0 copy-done
  7.9 1.6 %spectrum.1 = (f32[64,128]{1,0:T(8,128)S(1)}, f32[2,2,128]{2,1,0:T(2,128)S(1)}) custom-call(s32[1,64]{1,0:T(1,128)} %bitcast.31, f32[128,512]{1,0:T(8,128)S(1)} %copy-done, f32[2,2]{1,0:T(2,128)} %arm_ref.1, f32[3,128]{1,0:T(4,128)S(1)} %get-tuple-element.18.after_ref), custom_call_target="tpu_custom_call" | custom-call | tf_op jit(solution)/shard_map/spectrum/pallas_call | solution.py:168
  9.5 0.0 copy-start.1
  9.5 1.2 %collective-permute-done.1 = f32[4,3,128]{2,1,0:T(4,128)S(1)} collective-permute-done((f32[4,3,128]{2,1,0:T(4,128)S(1)}, f32[4,3,128]{2,1,0:T(4,128)S(1)}, u32[]{:S(2)}, u32[]{:S(2)}) %collective-permute-start.1) | collective-permute-done | bytes 6176 | tf_op jit(solution)/shard_map/ppermute | solution.py:18
  10.7 0.8 %collective-permute-start.2 = (f32[6,3,128]{2,1,0:T(4,128)S(1)}, f32[6,3,128]{2,1,0:T(4,128)S(1)}, u32[]{:S(2)}, u32[]{:S(2)}) collective-permute-start(f32[6,3,128]{2,1,0:T(4,128)S(1)} %pad_maximum_fusion), channel_id=1, source_target_pairs={{0,1},{1,0},{2,3},{3,2},{4,5},{5,4},{6,7},{7,6},{8,9},{9,8},{10,11... | collective-permute-start | bytes 27656 | tf_op jit(solution)/shard_map/ppermute | solution.py:18
  11.4 0.8 %collective-permute-done.2 = f32[6,3,128]{2,1,0:T(4,128)S(1)} collective-permute-done((f32[6,3,128]{2,1,0:T(4,128)S(1)}, f32[6,3,128]{2,1,0:T(4,128)S(1)}, u32[]{:S(2)}, u32[]{:S(2)}) %collective-permute-start.2) | collective-permute-done | bytes 9248 | tf_op jit(solution)/shard_map/ppermute | solution.py:18
  12.3 2.5 %collective-permute-start.5 = (f32[4,3,128]{2,1,0:T(4,128)S(1)}, f32[4,3,128]{2,1,0:T(4,128)S(1)}, u32[]{:S(2)}, u32[]{:S(2)}) collective-permute-start(f32[4,3,128]{2,1,0:T(4,128)S(1)} %slice_add_fusion), channel_id=1, source_target_pairs={{0,7},{1,6},{2,5},{3,4},{4,3},{5,2},{6,1},{7,0},{8,15},{9,14},{10,... | collective-permute-start | bytes 18440 | tf_op jit(solution)/shard_map/ppermute | solution.py:18
  14.8 0.2 %collective-permute-start.4 = (f32[4,3,128]{2,1,0:T(4,128)S(1)}, f32[4,3,128]{2,1,0:T(4,128)S(1)}, u32[]{:S(2)}, u32[]{:S(2)}) collective-permute-start(f32[4,3,128]{2,1,0:T(4,128)S(1)} %slice_add_fusion), channel_id=1, source_target_pairs={{0,5},{1,4},{2,7},{3,6},{4,1},{5,0},{6,3},{7,2},{8,13},{9,12},{10,... | collective-permute-start | bytes 18440 | tf_op jit(solution)/shard_map/ppermute | solution.py:18
  15.0 0.5 %collective-permute-start.3 = (f32[4,3,128]{2,1,0:T(4,128)S(1)}, f32[4,3,128]{2,1,0:T(4,128)S(1)}, u32[]{:S(2)}, u32[]{:S(2)}) collective-permute-start(f32[4,3,128]{2,1,0:T(4,128)S(1)} %slice_add_fusion), channel_id=1, source_target_pairs={{0,3},{1,2},{2,1},{3,0},{4,7},{5,6},{6,5},{7,4},{8,11},{9,10},{10,... | collective-permute-start | bytes 18440 | tf_op jit(solution)/shard_map/ppermute | solution.py:18
  15.4 0.8 %collective-permute-done.5 = f32[4,3,128]{2,1,0:T(4,128)S(1)} collective-permute-done((f32[4,3,128]{2,1,0:T(4,128)S(1)}, f32[4,3,128]{2,1,0:T(4,128)S(1)}, u32[]{:S(2)}, u32[]{:S(2)}) %collective-permute-start.5) | collective-permute-done | bytes 6176 | tf_op jit(solution)/shard_map/ppermute | solution.py:18
  16.3 1.6 %collective-permute-done.4 = f32[4,3,128]{2,1,0:T(4,128)S(1)} collective-permute-done((f32[4,3,128]{2,1,0:T(4,128)S(1)}, f32[4,3,128]{2,1,0:T(4,128)S(1)}, u32[]{:S(2)}, u32[]{:S(2)}) %collective-permute-start.4) | collective-permute-done | bytes 6176 | tf_op jit(solution)/shard_map/ppermute | solution.py:18
  17.8 0.2 %collective-permute-done.3 = f32[4,3,128]{2,1,0:T(4,128)S(1)} collective-permute-done((f32[4,3,128]{2,1,0:T(4,128)S(1)}, f32[4,3,128]{2,1,0:T(4,128)S(1)}, u32[]{:S(2)}, u32[]{:S(2)}) %collective-permute-start.3) | collective-permute-done | bytes 6176 | tf_op jit(solution)/shard_map/ppermute | solution.py:18
  18.1 0.0 copy-done.1
  18.1 1.2 %histories.1 = bf16[768,512]{1,0:T(8,128)(2,1)} custom-call(f32[2,3,128]{2,1,0:T(4,128)S(1)} %get-tuple-element.37.sym_ref, f32[2,3,128]{2,1,0:T(4,128)S(1)} %get-tuple-element.36.anti_ref, f32[2,2,128]{2,1,0:T(2,128)S(1)} %get-tuple-element.23.arm_ref, f32[64,128]{1,0:T(8,128)S(1)} %get-tuple-element.24.spec_ref, bf16[128,512]{1,0:T(8,128)(2,1)S(1)} %copy-done.1), custom_call_target="tpu_custom_call" | custom-call | tf_op jit(solution)/shard_map/histories/pallas_call | solution.py:203
  (13 shorter events, 0.1 us)
Async XLA Ops:
  0.7 5.7 %collective-permute-start = (f32[4,512]{1,0:T(4,128)S(1)}, f32[4,512]{1,0:T(4,128)S(1)}, u32[]{:S(2)}, u32[]{:S(2)}) collective-permute-start(f32[4,512]{1,0:T(4,128)S(1)} %pack.1.refs_2_), channel_id=1, source_target_pairs={{0,8},{1,9},{2,10},{3,11},{4,12},{5,13},{6,14},{7,15},{8,0},{9,1},... | collective-permute-start | bytes 24584 | tf_op jit(solution)/shard_map/ppermute | solution.py:18
  6.0 1.9 %copy-start = (f32[128,512]{1,0:T(8,128)S(1)}, f32[128,512]{1,0:T(8,128)}, u32[]{:S(2)}) copy-start(f32[128,512]{1,0:T(8,128)} %constant.18.clone.rows_ref) | copy-start | bytes 786436
  6.6 4.0 %collective-permute-start.1 = (f32[4,3,128]{2,1,0:T(4,128)S(1)}, f32[4,3,128]{2,1,0:T(4,128)S(1)}, u32[]{:S(2)}, u32[]{:S(2)}) collective-permute-start(f32[4,3,128]{2,1,0:T(4,128)S(1)} %pad_maximum_fusion.1), channel_id=1, source_target_pairs={{0,9},{1,8},{2,11},{3,10},{4,13},{5,12},{6,15},{7,14},{8,1},{9,0},... | collective-permute-start | bytes 18440 | tf_op jit(solution)/shard_map/ppermute | solution.py:18
  9.5 8.7 %copy-start.1 = (bf16[128,512]{1,0:T(8,128)(2,1)S(1)}, bf16[128,512]{1,0:T(8,128)(2,1)}, u32[]{:S(2)}) copy-start(bf16[128,512]{1,0:T(8,128)(2,1)} %constant.19.clone.basis_ref) | copy-start | bytes 393220
  10.7 1.6 %collective-permute-start.2 = (f32[6,3,128]{2,1,0:T(4,128)S(1)}, f32[6,3,128]{2,1,0:T(4,128)S(1)}, u32[]{:S(2)}, u32[]{:S(2)}) collective-permute-start(f32[6,3,128]{2,1,0:T(4,128)S(1)} %pad_maximum_fusion), channel_id=1, source_target_pairs={{0,1},{1,0},{2,3},{3,2},{4,5},{5,4},{6,7},{7,6},{8,9},{9,8},{10,11... | collective-permute-start | bytes 27656 | tf_op jit(solution)/shard_map/ppermute | solution.py:18
  12.3 4.0 %collective-permute-start.5 = (f32[4,3,128]{2,1,0:T(4,128)S(1)}, f32[4,3,128]{2,1,0:T(4,128)S(1)}, u32[]{:S(2)}, u32[]{:S(2)}) collective-permute-start(f32[4,3,128]{2,1,0:T(4,128)S(1)} %slice_add_fusion), channel_id=1, source_target_pairs={{0,7},{1,6},{2,5},{3,4},{4,3},{5,2},{6,1},{7,0},{8,15},{9,14},{10,... | collective-permute-start | bytes 18440 | tf_op jit(solution)/shard_map/ppermute | solution.py:18
  14.8 3.1 %collective-permute-start.4 = (f32[4,3,128]{2,1,0:T(4,128)S(1)}, f32[4,3,128]{2,1,0:T(4,128)S(1)}, u32[]{:S(2)}, u32[]{:S(2)}) collective-permute-start(f32[4,3,128]{2,1,0:T(4,128)S(1)} %slice_add_fusion), channel_id=1, source_target_pairs={{0,5},{1,4},{2,7},{3,6},{4,1},{5,0},{6,3},{7,2},{8,13},{9,12},{10,... | collective-permute-start | bytes 18440 | tf_op jit(solution)/shard_map/ppermute | solution.py:18
  15.0 3.1 %collective-permute-start.3 = (f32[4,3,128]{2,1,0:T(4,128)S(1)}, f32[4,3,128]{2,1,0:T(4,128)S(1)}, u32[]{:S(2)}, u32[]{:S(2)}) collective-permute-start(f32[4,3,128]{2,1,0:T(4,128)S(1)} %slice_add_fusion), channel_id=1, source_target_pairs={{0,3},{1,2},{2,1},{3,0},{4,7},{5,6},{6,5},{7,4},{8,11},{9,10},{10,... | collective-permute-start | bytes 18440 | tf_op jit(solution)/shard_map/ppermute | solution.py:18

commit v3 on v2

--- a/solution.py
+++ b/solution.py
@@ -60,9 +60,14 @@
     out_ref[3:4] = jnp.concatenate([ids[i : i + 1] for i in range(ids.shape[0])], 1)
 
 
-def sym_kernel(s_dev, sym_ref, anti_ref, geom_ref, total_ref, part_ref, held_ref):
-    rows = held_ref.shape[0]
-    held_ref[...] = anti_ref[...].reshape(held_ref.shape)
+def pack_kernel(geom_ref, ids_ref, out_ref):
+    ids = ids_ref[...].astype(jnp.float32)
+    out_ref[0:3] = geom_ref[...]
+    out_ref[3:4] = jnp.concatenate([ids[i : i + 1] for i in range(ids.shape[0])], 1)
+
+
+def sym_kernel(s_dev, sym_ref, geom_ref, total_ref, part_ref):
+    rows = 2 * sym_ref.shape[1]
     geom = geom_ref[...]
     sums = block_sums(sym_ref[...].reshape(rows, -1), geom, station_marks(geom[3:4], s_dev))
     for moment in range(3):
@@ -71,13 +76,23 @@
             part_ref[k, moment : moment + 1] = sums[moment][1 + k : 2 + k]
 
 
-def anti_kernel(s_dev, geom_ref, held_ref, total_ref, part_ref):
+def split_kernel(s_dev, geom_ref, weight_ref, marks_ref):
     geom = geom_ref[...]
-    sums = block_sums(held_ref[...], geom, station_marks(geom[3:4], s_dev))
+    weight_ref[...] = jnp.concatenate([geom[0:1], geom[0:1] * geom[1:2], geom[0:1] * geom[2:3]])
+    marks_ref[...] = station_marks(geom[3:4], s_dev)
+
+
+def anti_kernel(s_dev, weight_ref, marks_ref, anti_ref, total_ref, part_ref):
+    rows = 2 * anti_ref.shape[1]
+    press = anti_ref[...].reshape(rows, -1)
     for moment in range(3):
-        total_ref[moment : moment + 1] = sums[moment][0:1]
+        terms = (press * weight_ref[moment : moment + 1]).astype(jnp.bfloat16)
+        sums = lax.dot_general(
+            marks_ref[...], terms, (((1,), (1,)), ((), ())), preferred_element_type=jnp.float32
+        )
+        total_ref[moment : moment + 1] = sums[0:1]
         for k in range(s_dev):
-            part_ref[k, moment : moment + 1] = sums[moment][1 + k : 2 + k]
+            part_ref[k, moment : moment + 1] = sums[1 + k : 2 + k]
 
 
 def spectrum_kernel(index_ref, rows_ref, arm_ref, after_ref, spec_ref, arms_ref):
@@ -150,24 +165,23 @@
 
     ids = box_station.reshape(-1, LANES)
     geom = pl.pallas_call(pack_kernel, out_shape=pltpu.VMEM((4, box_dev), f32), name="pack")(box_geom, ids)
-    partner_geom = swap(geom, "box", half)
-    sym_total, sym_part, held = pl.pallas_call(
+    far_geom = swap(geom, "box", half ^ 1)
+    near_anti = swap(anti_press, "box", 1)
+    sym_total, sym_part = pl.pallas_call(
         lambda *refs: sym_kernel(s_dev, *refs),
-        out_shape=(
-            pltpu.VMEM((3, wide), f32),
-            pltpu.VMEM((s_dev, 3, wide), f32),
-            pltpu.VMEM((wide, box_dev), f32),
-        ),
+        out_shape=(pltpu.VMEM((3, wide), f32), pltpu.VMEM((s_dev, 3, wide), f32)),
         name="sym_sums",
-    )(sym_press, anti_press, in_vmem(geom))
+    )(sym_press, in_vmem(geom))
+    weight, marks = pl.pallas_call(
+        lambda *refs: split_kernel(s_dev, *refs),
+        out_shape=(pltpu.VMEM((3, box_dev), f32), pltpu.VMEM((8, box_dev), jnp.bfloat16)),
+        name="weights",
+    )(in_vmem(far_geom))
     anti_total, anti_part = pl.pallas_call(
         lambda *refs: anti_kernel(s_dev, *refs), out_shape=(pltpu.VMEM((3, wide), f32),pltpu.VMEM((s_dev, 3, wide), f32)), name="anti_sums"
-    )(in_vmem(partner_geom), in_vmem(held))
+    )(in_vmem(weight), in_vmem(marks), in_vmem(near_anti))
 
     rows = fourier_rows(freqs, NFFT)
-    spec, arm = pl.pallas_call(
-        spectrum_kernel, out_shape=(pltpu.VMEM((gusts, wide), f32), pltpu.VMEM((2, s_dev, wide), f32)), name="spectrum"
-    )(gust_index.reshape(1, gusts), in_vmem(jnp.asarray(rows)), station_geom, in_vmem(anti_total))
     scale = np.where(np.arange(wide) % freqs == 0, 1.0, 2.0)[:, None] / NFFT
     basis = jnp.asarray((rows * scale).astype(np.float32).astype(jnp.bfloat16))
 
@@ -177,16 +191,19 @@
     is_low = (me < half).astype(f32)
     past = jnp.stack([got[0], anti_total]) * is_low
     total = jnp.stack([sym_total, got[1]])
-    past, spec, arm = lax.optimization_barrier((past, spec, arm))
     state = jnp.concatenate([past, total])
 
     def later(mask):
         return ((me ^ mask) > me).astype(f32)
 
-    got = swap(jnp.concatenate([state, got[2:]]), "box", 1)
+    anti_part = got[2:]
+    got = swap(state, "box", 1)
     sym_part = sym_part + later(1) * got[2]
-    anti_part = got[4:] + later(1) * total[1]
-    state = state + got[:4]
+    anti_part = anti_part + later(1) * got[3]
+    state = state + got
+    spec, arm = pl.pallas_call(
+        spectrum_kernel, out_shape=(pltpu.VMEM((gusts, wide), f32), pltpu.VMEM((2, s_dev, wide), f32)), name="spectrum"
+    )(gust_index.reshape(1, gusts), in_vmem(jnp.asarray(rows)), station_geom, in_vmem(state))
     low, high = 1, half.bit_length() - 1
     while low < high:
         size = min(2, high - low)

time: 19.6 us -> 19.2 us (0.980)
  waiting for transfers between devices: 4.95 us -> 3.87 us
  starting transfers between devices: 9.22 us -> 9.98 us
    ppermute x6 -> x7, waiting for transfers between devices: 4.95 us -> 3.87 us  [swap(): return lax.ppermute(block, axis, [(i, i ^ mask) for i in range(count)])]
    ppermute x6 -> x7, starting transfers between devices: 9.22 us -> 9.98 us  [swap(): return lax.ppermute(block, axis, [(i, i ^ mask) for i in range(count)])]
  transfers between devices with their start and end apart: 6 -> 7, of which waited for: 6 -> 5; matrix products, arithmetic and copies ran while one was open for 0% -> 0% of each run, Pallas kernels for 15% -> 19%
where the time goes in v3:
time: 19.2 us; the launch traced here: 19 us
  starting transfers between devices  9.98 us (52%)
  Pallas kernels  4.93 us (26%)
  waiting for transfers between devices  3.87 us (20%)
    ppermute x7, starting transfers between devices, swap(): return lax.ppermute(block, axis, [(i, i ^ mask) for i in range(count)])  9.98 us
    ppermute x7, waiting for transfers between devices, swap(): return lax.ppermute(block, axis, [(i, i ^ mask) for i in range(count)])  3.87 us
    pallas_call x1, Pallas kernels, on_device(): pl.pallas_call(spectrum_kernel, out_shape=(pltpu.VMEM((gusts, wide), f32)...  1.58 us
    pallas_call x1, Pallas kernels, on_device(): pl.pallas_call(lambda *refs: sym_kernel(s_dev, *refs), out_shape=(pltpu.V...  1.19 us
    pallas_call x1, Pallas kernels, on_device(): pl.pallas_call(history_kernel, out_shape=jax.ShapeDtypeStruct((s_dev * 6...  1.17 us
    pallas_call x1, Pallas kernels, on_device(): pl.pallas_call(pack_kernel, out_shape=pltpu.VMEM((4, box_dev), f32), name...  0.71 us
  transfers between devices with their start and end apart: 7, of which 5 were waited for; matrix products, arithmetic and copies ran while one was open for 0% of the time, Pallas kernels for 19%

profile of v3, /device:TPU:0, one launch (start us, length us, event | category | flops | bytes accessed | tf_op | source)
XLA Modules:
  0.0 19.0 jit_solution(13261480945521141608)
XLA Ops:
  0.0 0.5 %collective-permute-start.1 = (f32[2,64,512]{2,1,0:T(8,128)}, f32[2,64,512]{2,1,0:T(8,128)S(1)}, u32[]{:S(2)}, u32[]{:S(2)}) collective-permute-start(f32[2,64,512]{2,1,0:T(8,128)} %param.9), channel_id=1, source_target_pairs={{0,1},{1,0},{2,3},{3,2},{4,5},{5,4},{6,7},{7,6},{8,9},{9,8},{10,11... | collective-permute-start | bytes 786440 | tf_op jit(solution)/shard_map/ppermute | solution.py:18
  0.5 0.7 %pack.1.refs_1_ = f32[4,512]{1,0:T(4,128)S(1)} custom-call(f32[3,512]{1,0:T(4,128)} %geom_ref.1, s32[4,128]{1,0:T(4,128)} %bitcast.30), custom_call_target="tpu_custom_call" | custom-call | tf_op jit(solution)/shard_map/pack/pallas_call | solution.py:167
  1.2 3.7 %collective-permute-start = (f32[4,512]{1,0:T(4,128)S(1)}, f32[4,512]{1,0:T(4,128)S(1)}, u32[]{:S(2)}, u32[]{:S(2)}) collective-permute-start(f32[4,512]{1,0:T(4,128)S(1)} %pack.1.refs_1_), channel_id=1, source_target_pairs={{0,9},{1,8},{2,11},{3,10},{4,13},{5,12},{6,15},{7,14},{8,1},{9,0},... | collective-permute-start | bytes 24584 | tf_op jit(solution)/shard_map/ppermute | solution.py:18
  4.9 1.2 %sym_sums.1 = (f32[3,128]{1,0:T(4,128)S(1)}, f32[2,3,128]{2,1,0:T(4,128)S(1)}) custom-call(f32[2,64,512]{2,1,0:T(8,128)} %refs_0_.1, f32[4,512]{1,0:T(4,128)S(1)} %pack.1.refs_1_), custom_call_target="tpu_custom_call" | custom-call | tf_op jit(solution)/shard_map/sym_sums/pallas_call | solution.py:170
  6.1 0.0 copy-start
  6.1 0.2 collective-permute-done.refs_0_
  6.2 0.1 weights.1
  6.3 0.0 collective-permute-done.1.refs_2_
  6.3 0.2 %anti_sums.1 = (f32[3,128]{1,0:T(4,128)S(1)}, f32[2,3,128]{2,1,0:T(4,128)S(1)}) custom-call(f32[3,512]{1,0:T(4,128)S(1)} %get-tuple-element.15.refs_0_, bf16[8,512]{1,0:T(8,128)(2,1)S(1)} %get-tuple-element.16.refs_1_, f32[2,64,512]{2,1,0:T(8,128)S(1)} %collective-permute-done.1.refs_2_), custom_call_target="tpu_custom_call" | custom-call | tf_op jit(solution)/shard_map/anti_sums/pallas_call | solution.py:180
  6.5 2.7 %collective-permute-start.2 = (f32[4,3,128]{2,1,0:T(4,128)S(1)}, f32[4,3,128]{2,1,0:T(4,128)S(1)}, u32[]{:S(2)}, u32[]{:S(2)}) collective-permute-start(f32[4,3,128]{2,1,0:T(4,128)S(1)} %pad_maximum_fusion), channel_id=1, source_target_pairs={{0,9},{1,8},{2,11},{3,10},{4,13},{5,12},{6,15},{7,14},{8,1},{9,0},... | collective-permute-start | bytes 18440 | tf_op jit(solution)/shard_map/ppermute | solution.py:18
  9.2 1.4 %collective-permute-done.2 = f32[4,3,128]{2,1,0:T(4,128)S(1)} collective-permute-done((f32[4,3,128]{2,1,0:T(4,128)S(1)}, f32[4,3,128]{2,1,0:T(4,128)S(1)}, u32[]{:S(2)}, u32[]{:S(2)}) %collective-permute-start.2) | collective-permute-done | bytes 6176 | tf_op jit(solution)/shard_map/ppermute | solution.py:18
  10.6 0.2 collective-permute-start.3
  10.8 1.1 %collective-permute-done.3 = f32[4,3,128]{2,1,0:T(4,128)S(1)} collective-permute-done((f32[4,3,128]{2,1,0:T(4,128)S(1)}, f32[4,3,128]{2,1,0:T(4,128)S(1)}, u32[]{:S(2)}, u32[]{:S(2)}) %collective-permute-start.3) | collective-permute-done | bytes 6176 | tf_op jit(solution)/shard_map/ppermute | solution.py:18
  11.8 2.6 %collective-permute-start.6 = (f32[4,3,128]{2,1,0:T(4,128)S(1)}, f32[4,3,128]{2,1,0:T(4,128)S(1)}, u32[]{:S(2)}, u32[]{:S(2)}) collective-permute-start(f32[4,3,128]{2,1,0:T(4,128)S(1)} %fusion.12.after_ref), channel_id=1, source_target_pairs={{0,7},{1,6},{2,5},{3,4},{4,3},{5,2},{6,1},{7,0},{8,15},{9,14},{10,... | collective-permute-start | bytes 18440 | tf_op jit(solution)/shard_map/ppermute | solution.py:18
  14.4 0.2 %collective-permute-start.5 = (f32[4,3,128]{2,1,0:T(4,128)S(1)}, f32[4,3,128]{2,1,0:T(4,128)S(1)}, u32[]{:S(2)}, u32[]{:S(2)}) collective-permute-start(f32[4,3,128]{2,1,0:T(4,128)S(1)} %fusion.12.after_ref), channel_id=1, source_target_pairs={{0,5},{1,4},{2,7},{3,6},{4,1},{5,0},{6,3},{7,2},{8,13},{9,12},{10,... | collective-permute-start | bytes 18440 | tf_op jit(solution)/shard_map/ppermute | solution.py:18
  14.6 0.2 %collective-permute-start.4 = (f32[4,3,128]{2,1,0:T(4,128)S(1)}, f32[4,3,128]{2,1,0:T(4,128)S(1)}, u32[]{:S(2)}, u32[]{:S(2)}) collective-permute-start(f32[4,3,128]{2,1,0:T(4,128)S(1)} %fusion.12.after_ref), channel_id=1, source_target_pairs={{0,3},{1,2},{2,1},{3,0},{4,7},{5,6},{6,5},{7,4},{8,11},{9,10},{10,... | collective-permute-start | bytes 18440 | tf_op jit(solution)/shard_map/ppermute | solution.py:18
  14.8 0.0 copy-done
  14.8 1.6 %spectrum.1 = (f32[64,128]{1,0:T(8,128)S(1)}, f32[2,2,128]{2,1,0:T(2,128)S(1)}) custom-call(s32[1,64]{1,0:T(1,128)} %bitcast.31, f32[128,512]{1,0:T(8,128)S(1)} %copy-done, f32[2,2]{1,0:T(2,128)} %arm_ref.1, f32[4,3,128]{2,1,0:T(4,128)S(1)} %fusion.12.after_ref), custom_call_target="tpu_custom_call" | custom-call | tf_op jit(solution)/shard_map/spectrum/pallas_call | solution.py:204
  16.4 0.0 copy-start.1
  16.4 0.0 collective-permute-done.6
  16.4 1.0 %collective-permute-done.5 = f32[4,3,128]{2,1,0:T(4,128)S(1)} collective-permute-done((f32[4,3,128]{2,1,0:T(4,128)S(1)}, f32[4,3,128]{2,1,0:T(4,128)S(1)}, u32[]{:S(2)}, u32[]{:S(2)}) %collective-permute-start.5) | collective-permute-done | bytes 6176 | tf_op jit(solution)/shard_map/ppermute | solution.py:18
  17.5 0.2 %collective-permute-done.4 = f32[4,3,128]{2,1,0:T(4,128)S(1)} collective-permute-done((f32[4,3,128]{2,1,0:T(4,128)S(1)}, f32[4,3,128]{2,1,0:T(4,128)S(1)}, u32[]{:S(2)}, u32[]{:S(2)}) %collective-permute-start.4) | collective-permute-done | bytes 6176 | tf_op jit(solution)/shard_map/ppermute | solution.py:18
  17.8 0.0 copy-done.1
  17.8 1.2 %histories.1 = bf16[768,512]{1,0:T(8,128)(2,1)} custom-call(f32[2,3,128]{2,1,0:T(4,128)S(1)} %get-tuple-element.34.sym_ref, f32[2,3,128]{2,1,0:T(4,128)S(1)} %get-tuple-element.33.anti_ref, f32[2,2,128]{2,1,0:T(2,128)S(1)} %get-tuple-element.19.arm_ref, f32[64,128]{1,0:T(8,128)S(1)} %get-tuple-element.20.spec_ref, bf16[128,512]{1,0:T(8,128)(2,1)S(1)} %copy-done.1), custom_call_target="tpu_custom_call" | custom-call | tf_op jit(solution)/shard_map/histories/pallas_call | solution.py:220
  (12 shorter events, 0.1 us)
Async XLA Ops:
  0.0 6.3 %collective-permute-start.1 = (f32[2,64,512]{2,1,0:T(8,128)}, f32[2,64,512]{2,1,0:T(8,128)S(1)}, u32[]{:S(2)}, u32[]{:S(2)}) collective-permute-start(f32[2,64,512]{2,1,0:T(8,128)} %param.9), channel_id=1, source_target_pairs={{0,1},{1,0},{2,3},{3,2},{4,5},{5,4},{6,7},{7,6},{8,9},{9,8},{10,11... | collective-permute-start | bytes 786440 | tf_op jit(solution)/shard_map/ppermute | solution.py:18
  1.2 5.1 %collective-permute-start = (f32[4,512]{1,0:T(4,128)S(1)}, f32[4,512]{1,0:T(4,128)S(1)}, u32[]{:S(2)}, u32[]{:S(2)}) collective-permute-start(f32[4,512]{1,0:T(4,128)S(1)} %pack.1.refs_1_), channel_id=1, source_target_pairs={{0,9},{1,8},{2,11},{3,10},{4,13},{5,12},{6,15},{7,14},{8,1},{9,0},... | collective-permute-start | bytes 24584 | tf_op jit(solution)/shard_map/ppermute | solution.py:18
  6.1 8.8 %copy-start = (f32[128,512]{1,0:T(8,128)S(1)}, f32[128,512]{1,0:T(8,128)}, u32[]{:S(2)}) copy-start(f32[128,512]{1,0:T(8,128)} %constant.19.clone.rows_ref) | copy-start | bytes 786436
  6.5 4.0 %collective-permute-start.2 = (f32[4,3,128]{2,1,0:T(4,128)S(1)}, f32[4,3,128]{2,1,0:T(4,128)S(1)}, u32[]{:S(2)}, u32[]{:S(2)}) collective-permute-start(f32[4,3,128]{2,1,0:T(4,128)S(1)} %pad_maximum_fusion), channel_id=1, source_target_pairs={{0,9},{1,8},{2,11},{3,10},{4,13},{5,12},{6,15},{7,14},{8,1},{9,0},... | collective-permute-start | bytes 18440 | tf_op jit(solution)/shard_map/ppermute | solution.py:18
  10.6 1.2 %collective-permute-start.3 = (f32[4,3,128]{2,1,0:T(4,128)S(1)}, f32[4,3,128]{2,1,0:T(4,128)S(1)}, u32[]{:S(2)}, u32[]{:S(2)}) collective-permute-start(f32[4,3,128]{2,1,0:T(4,128)S(1)} %pad_maximum_fusion.1), channel_id=1, source_target_pairs={{0,1},{1,0},{2,3},{3,2},{4,5},{5,4},{6,7},{7,6},{8,9},{9,8},{10,11... | collective-permute-start | bytes 18440 | tf_op jit(solution)/shard_map/ppermute | solution.py:18
  11.8 4.6 %collective-permute-start.6 = (f32[4,3,128]{2,1,0:T(4,128)S(1)}, f32[4,3,128]{2,1,0:T(4,128)S(1)}, u32[]{:S(2)}, u32[]{:S(2)}) collective-permute-start(f32[4,3,128]{2,1,0:T(4,128)S(1)} %fusion.12.after_ref), channel_id=1, source_target_pairs={{0,7},{1,6},{2,5},{3,4},{4,3},{5,2},{6,1},{7,0},{8,15},{9,14},{10,... | collective-permute-start | bytes 18440 | tf_op jit(solution)/shard_map/ppermute | solution.py:18
  14.4 3.1 %collective-permute-start.5 = (f32[4,3,128]{2,1,0:T(4,128)S(1)}, f32[4,3,128]{2,1,0:T(4,128)S(1)}, u32[]{:S(2)}, u32[]{:S(2)}) collective-permute-start(f32[4,3,128]{2,1,0:T(4,128)S(1)} %fusion.12.after_ref), channel_id=1, source_target_pairs={{0,5},{1,4},{2,7},{3,6},{4,1},{5,0},{6,3},{7,2},{8,13},{9,12},{10,... | collective-permute-start | bytes 18440 | tf_op jit(solution)/shard_map/ppermute | solution.py:18
  14.6 3.1 %collective-permute-start.4 = (f32[4,3,128]{2,1,0:T(4,128)S(1)}, f32[4,3,128]{2,1,0:T(4,128)S(1)}, u32[]{:S(2)}, u32[]{:S(2)}) collective-permute-start(f32[4,3,128]{2,1,0:T(4,128)S(1)} %fusion.12.after_ref), channel_id=1, source_target_pairs={{0,3},{1,2},{2,1},{3,0},{4,7},{5,6},{6,5},{7,4},{8,11},{9,10},{10,... | collective-permute-start | bytes 18440 | tf_op jit(solution)/shard_map/ppermute | solution.py:18
  16.4 1.4 %copy-start.1 = (bf16[128,512]{1,0:T(8,128)(2,1)S(1)}, bf16[128,512]{1,0:T(8,128)(2,1)}, u32[]{:S(2)}) copy-start(bf16[128,512]{1,0:T(8,128)(2,1)} %constant.18.clone.basis_ref) | copy-start | bytes 393220

commit v4 on v3

--- a/solution.py
+++ b/solution.py
@@ -76,23 +76,14 @@
             part_ref[k, moment : moment + 1] = sums[moment][1 + k : 2 + k]
 
 
-def split_kernel(s_dev, geom_ref, weight_ref, marks_ref):
+def anti_kernel(s_dev, geom_ref, anti_ref, sym_ref, sent_ref):
     geom = geom_ref[...]
-    weight_ref[...] = jnp.concatenate([geom[0:1], geom[0:1] * geom[1:2], geom[0:1] * geom[2:3]])
-    marks_ref[...] = station_marks(geom[3:4], s_dev)
-
-
-def anti_kernel(s_dev, weight_ref, marks_ref, anti_ref, total_ref, part_ref):
     rows = 2 * anti_ref.shape[1]
-    press = anti_ref[...].reshape(rows, -1)
+    sums = block_sums(anti_ref[...].reshape(rows, -1), geom, station_marks(geom[3:4], s_dev))
+    sent_ref[0] = sym_ref[...]
     for moment in range(3):
-        terms = (press * weight_ref[moment : moment + 1]).astype(jnp.bfloat16)
-        sums = lax.dot_general(
-            marks_ref[...], terms, (((1,), (1,)), ((), ())), preferred_element_type=jnp.float32
-        )
-        total_ref[moment : moment + 1] = sums[0:1]
-        for k in range(s_dev):
-            part_ref[k, moment : moment + 1] = sums[1 + k : 2 + k]
+        for k in range(1 + s_dev):
+            sent_ref[1 + k, moment : moment + 1] = sums[moment][k : k + 1]
 
 
 def spectrum_kernel(index_ref, rows_ref, arm_ref, after_ref, spec_ref, arms_ref):
@@ -172,24 +163,20 @@
         out_shape=(pltpu.VMEM((3, wide), f32), pltpu.VMEM((s_dev, 3, wide), f32)),
         name="sym_sums",
     )(sym_press, in_vmem(geom))
-    weight, marks = pl.pallas_call(
-        lambda *refs: split_kernel(s_dev, *refs),
-        out_shape=(pltpu.VMEM((3, box_dev), f32), pltpu.VMEM((8, box_dev), jnp.bfloat16)),
-        name="weights",
-    )(in_vmem(far_geom))
-    anti_total, anti_part = pl.pallas_call(
-        lambda *refs: anti_kernel(s_dev, *refs), out_shape=(pltpu.VMEM((3, wide), f32),pltpu.VMEM((s_dev, 3, wide), f32)), name="anti_sums"
-    )(in_vmem(weight), in_vmem(marks), in_vmem(near_anti))
+    sent = pl.pallas_call(
+        lambda *refs: anti_kernel(s_dev, *refs),
+        out_shape=pltpu.VMEM((2 + s_dev, 3, wide), f32),
+        name="anti_sums",
+    )(in_vmem(far_geom), in_vmem(near_anti), in_vmem(sym_total))
 
     rows = fourier_rows(freqs, NFFT)
     scale = np.where(np.arange(wide) % freqs == 0, 1.0, 2.0)[:, None] / NFFT
     basis = jnp.asarray((rows * scale).astype(np.float32).astype(jnp.bfloat16))
 
 
-    sent = jnp.concatenate([jnp.stack([sym_total, anti_total]), anti_part])
     got = swap(sent, "box", half ^ 1)
     is_low = (me < half).astype(f32)
-    past = jnp.stack([got[0], anti_total]) * is_low
+    past = jnp.stack([got[0], sent[1]]) * is_low
     total = jnp.stack([sym_total, got[1]])
     state = jnp.concatenate([past, total])
 

time: 19.2 us -> 19.1 us (level)
  no operation moved by 1% of the time
where the time goes in v4:
time: 19.1 us; the launch traced here: 18.8 us
  starting transfers between devices  9.93 us (52%)
  Pallas kernels  4.89 us (26%)
  waiting for transfers between devices  3.86 us (20%)
    ppermute x7, starting transfers between devices, swap(): return lax.ppermute(block, axis, [(i, i ^ mask) for i in range(count)])  9.93 us
    ppermute x7, waiting for transfers between devices, swap(): return lax.ppermute(block, axis, [(i, i ^ mask) for i in range(count)])  3.86 us
    pallas_call x1, Pallas kernels, on_device(): pl.pallas_call(spectrum_kernel, out_shape=(pltpu.VMEM((gusts, wide), f32)...  1.58 us
    pallas_call x1, Pallas kernels, on_device(): pl.pallas_call(lambda *refs: sym_kernel(s_dev, *refs), out_shape=(pltpu.V...  1.19 us
    pallas_call x1, Pallas kernels, on_device(): pl.pallas_call(history_kernel, out_shape=jax.ShapeDtypeStruct((s_dev * 6...  1.17 us
    pallas_call x1, Pallas kernels, on_device(): pl.pallas_call(pack_kernel, out_shape=pltpu.VMEM((4, box_dev), f32), name...  0.71 us
  transfers between devices with their start and end apart: 7, of which 5 were waited for; matrix products, arithmetic and copies ran while one was open for 0% of the time, Pallas kernels for 19%

profile of v4, /device:TPU:0, one launch (start us, length us, event | category | flops | bytes accessed | tf_op | source)
XLA Modules:
  0.0 18.8 jit_solution(6768133032985016895)
XLA Ops:
  0.0 0.5 %collective-permute-start.1 = (f32[2,64,512]{2,1,0:T(8,128)}, f32[2,64,512]{2,1,0:T(8,128)S(1)}, u32[]{:S(2)}, u32[]{:S(2)}) collective-permute-start(f32[2,64,512]{2,1,0:T(8,128)} %param.9), channel_id=1, source_target_pairs={{0,1},{1,0},{2,3},{3,2},{4,5},{5,4},{6,7},{7,6},{8,9},{9,8},{10,11... | collective-permute-start | bytes 786440 | tf_op jit(solution)/shard_map/ppermute | solution.py:18
  0.5 0.7 %pack.1.refs_1_ = f32[4,512]{1,0:T(4,128)S(1)} custom-call(f32[3,512]{1,0:T(4,128)} %geom_ref.1, s32[4,128]{1,0:T(4,128)} %bitcast.26), custom_call_target="tpu_custom_call" | custom-call | tf_op jit(solution)/shard_map/pack/pallas_call | solution.py:158
  1.2 3.7 %collective-permute-start = (f32[4,512]{1,0:T(4,128)S(1)}, f32[4,512]{1,0:T(4,128)S(1)}, u32[]{:S(2)}, u32[]{:S(2)}) collective-permute-start(f32[4,512]{1,0:T(4,128)S(1)} %pack.1.refs_1_), channel_id=1, source_target_pairs={{0,9},{1,8},{2,11},{3,10},{4,13},{5,12},{6,15},{7,14},{8,1},{9,0},... | collective-permute-start | bytes 24584 | tf_op jit(solution)/shard_map/ppermute | solution.py:18
  4.9 1.2 %sym_sums.1 = (f32[3,128]{1,0:T(4,128)S(1)}, f32[2,3,128]{2,1,0:T(4,128)S(1)}) custom-call(f32[2,64,512]{2,1,0:T(8,128)} %refs_0_.1, f32[4,512]{1,0:T(4,128)S(1)} %pack.1.refs_1_), custom_call_target="tpu_custom_call" | custom-call | tf_op jit(solution)/shard_map/sym_sums/pallas_call | solution.py:161
  6.1 0.0 copy-start
  6.1 0.2 collective-permute-done.refs_0_
  6.2 0.0 collective-permute-done.1.refs_1_
  6.2 0.2 %anti_sums.1 = f32[4,3,128]{2,1,0:T(4,128)S(1)} custom-call(f32[4,512]{1,0:T(4,128)S(1)} %collective-permute-done.refs_0_, f32[2,64,512]{2,1,0:T(8,128)S(1)} %collective-permute-done.1.refs_1_, f32[3,128]{1,0:T(4,128)S(1)} %get-tuple-element.10.refs_2_), custom_call_target="tpu_custom_call" | custom-call | tf_op jit(solution)/shard_map/anti_sums/pallas_call | solution.py:166
  6.5 2.6 %collective-permute-start.2 = (f32[4,3,128]{2,1,0:T(4,128)S(1)}, f32[4,3,128]{2,1,0:T(4,128)S(1)}, u32[]{:S(2)}, u32[]{:S(2)}) collective-permute-start(f32[4,3,128]{2,1,0:T(4,128)S(1)} %anti_sums.1), channel_id=1, source_target_pairs={{0,9},{1,8},{2,11},{3,10},{4,13},{5,12},{6,15},{7,14},{8,1},{9,0},... | collective-permute-start | bytes 18440 | tf_op jit(solution)/shard_map/ppermute | solution.py:18
  9.1 1.4 %collective-permute-done.2 = f32[4,3,128]{2,1,0:T(4,128)S(1)} collective-permute-done((f32[4,3,128]{2,1,0:T(4,128)S(1)}, f32[4,3,128]{2,1,0:T(4,128)S(1)}, u32[]{:S(2)}, u32[]{:S(2)}) %collective-permute-start.2) | collective-permute-done | bytes 6176 | tf_op jit(solution)/shard_map/ppermute | solution.py:18
  10.5 0.2 collective-permute-start.3
  10.7 1.1 %collective-permute-done.3 = f32[4,3,128]{2,1,0:T(4,128)S(1)} collective-permute-done((f32[4,3,128]{2,1,0:T(4,128)S(1)}, f32[4,3,128]{2,1,0:T(4,128)S(1)}, u32[]{:S(2)}, u32[]{:S(2)}) %collective-permute-start.3) | collective-permute-done | bytes 6176 | tf_op jit(solution)/shard_map/ppermute | solution.py:18
  11.7 2.6 %collective-permute-start.6 = (f32[4,3,128]{2,1,0:T(4,128)S(1)}, f32[4,3,128]{2,1,0:T(4,128)S(1)}, u32[]{:S(2)}, u32[]{:S(2)}) collective-permute-start(f32[4,3,128]{2,1,0:T(4,128)S(1)} %fusion.12.after_ref), channel_id=1, source_target_pairs={{0,7},{1,6},{2,5},{3,4},{4,3},{5,2},{6,1},{7,0},{8,15},{9,14},{10,... | collective-permute-start | bytes 18440 | tf_op jit(solution)/shard_map/ppermute | solution.py:18
  14.3 0.2 %collective-permute-start.5 = (f32[4,3,128]{2,1,0:T(4,128)S(1)}, f32[4,3,128]{2,1,0:T(4,128)S(1)}, u32[]{:S(2)}, u32[]{:S(2)}) collective-permute-start(f32[4,3,128]{2,1,0:T(4,128)S(1)} %fusion.12.after_ref), channel_id=1, source_target_pairs={{0,5},{1,4},{2,7},{3,6},{4,1},{5,0},{6,3},{7,2},{8,13},{9,12},{10,... | collective-permute-start | bytes 18440 | tf_op jit(solution)/shard_map/ppermute | solution.py:18
  14.5 0.2 %collective-permute-start.4 = (f32[4,3,128]{2,1,0:T(4,128)S(1)}, f32[4,3,128]{2,1,0:T(4,128)S(1)}, u32[]{:S(2)}, u32[]{:S(2)}) collective-permute-start(f32[4,3,128]{2,1,0:T(4,128)S(1)} %fusion.12.after_ref), channel_id=1, source_target_pairs={{0,3},{1,2},{2,1},{3,0},{4,7},{5,6},{6,5},{7,4},{8,11},{9,10},{10,... | collective-permute-start | bytes 18440 | tf_op jit(solution)/shard_map/ppermute | solution.py:18
  14.7 0.0 copy-done
  14.7 1.6 %spectrum.1 = (f32[64,128]{1,0:T(8,128)S(1)}, f32[2,2,128]{2,1,0:T(2,128)S(1)}) custom-call(s32[1,64]{1,0:T(1,128)} %bitcast.27, f32[128,512]{1,0:T(8,128)S(1)} %copy-done, f32[2,2]{1,0:T(2,128)} %arm_ref.1, f32[4,3,128]{2,1,0:T(4,128)S(1)} %fusion.12.after_ref), custom_call_target="tpu_custom_call" | custom-call | tf_op jit(solution)/shard_map/spectrum/pallas_call | solution.py:191
  16.3 0.0 copy-start.1
  16.3 0.0 collective-permute-done.6
  16.3 1.0 %collective-permute-done.5 = f32[4,3,128]{2,1,0:T(4,128)S(1)} collective-permute-done((f32[4,3,128]{2,1,0:T(4,128)S(1)}, f32[4,3,128]{2,1,0:T(4,128)S(1)}, u32[]{:S(2)}, u32[]{:S(2)}) %collective-permute-start.5) | collective-permute-done | bytes 6176 | tf_op jit(solution)/shard_map/ppermute | solution.py:18
  17.4 0.2 %collective-permute-done.4 = f32[4,3,128]{2,1,0:T(4,128)S(1)} collective-permute-done((f32[4,3,128]{2,1,0:T(4,128)S(1)}, f32[4,3,128]{2,1,0:T(4,128)S(1)}, u32[]{:S(2)}, u32[]{:S(2)}) %collective-permute-start.4) | collective-permute-done | bytes 6176 | tf_op jit(solution)/shard_map/ppermute | solution.py:18
  17.7 0.0 copy-done.1
  17.7 1.2 %histories.1 = bf16[768,512]{1,0:T(8,128)(2,1)} custom-call(f32[2,3,128]{2,1,0:T(4,128)S(1)} %get-tuple-element.26.sym_ref, f32[2,3,128]{2,1,0:T(4,128)S(1)} %get-tuple-element.25.anti_ref, f32[2,2,128]{2,1,0:T(2,128)S(1)} %get-tuple-element.11.arm_ref, f32[64,128]{1,0:T(8,128)S(1)} %get-tuple-element.12.spec_ref, bf16[128,512]{1,0:T(8,128)(2,1)S(1)} %copy-done.1), custom_call_target="tpu_custom_call" | custom-call | tf_op jit(solution)/shard_map/histories/pallas_call | solution.py:207
  (12 shorter events, 0.1 us)
Async XLA Ops:
  0.0 6.2 %collective-permute-start.1 = (f32[2,64,512]{2,1,0:T(8,128)}, f32[2,64,512]{2,1,0:T(8,128)S(1)}, u32[]{:S(2)}, u32[]{:S(2)}) collective-permute-start(f32[2,64,512]{2,1,0:T(8,128)} %param.9), channel_id=1, source_target_pairs={{0,1},{1,0},{2,3},{3,2},{4,5},{5,4},{6,7},{7,6},{8,9},{9,8},{10,11... | collective-permute-start | bytes 786440 | tf_op jit(solution)/shard_map/ppermute | solution.py:18
  1.2 5.1 %collective-permute-start = (f32[4,512]{1,0:T(4,128)S(1)}, f32[4,512]{1,0:T(4,128)S(1)}, u32[]{:S(2)}, u32[]{:S(2)}) collective-permute-start(f32[4,512]{1,0:T(4,128)S(1)} %pack.1.refs_1_), channel_id=1, source_target_pairs={{0,9},{1,8},{2,11},{3,10},{4,13},{5,12},{6,15},{7,14},{8,1},{9,0},... | collective-permute-start | bytes 24584 | tf_op jit(solution)/shard_map/ppermute | solution.py:18
  6.1 8.7 %copy-start = (f32[128,512]{1,0:T(8,128)S(1)}, f32[128,512]{1,0:T(8,128)}, u32[]{:S(2)}) copy-start(f32[128,512]{1,0:T(8,128)} %constant.19.clone.rows_ref) | copy-start | bytes 786436
  6.5 4.0 %collective-permute-start.2 = (f32[4,3,128]{2,1,0:T(4,128)S(1)}, f32[4,3,128]{2,1,0:T(4,128)S(1)}, u32[]{:S(2)}, u32[]{:S(2)}) collective-permute-start(f32[4,3,128]{2,1,0:T(4,128)S(1)} %anti_sums.1), channel_id=1, source_target_pairs={{0,9},{1,8},{2,11},{3,10},{4,13},{5,12},{6,15},{7,14},{8,1},{9,0},... | collective-permute-start | bytes 18440 | tf_op jit(solution)/shard_map/ppermute | solution.py:18
  10.5 1.2 %collective-permute-start.3 = (f32[4,3,128]{2,1,0:T(4,128)S(1)}, f32[4,3,128]{2,1,0:T(4,128)S(1)}, u32[]{:S(2)}, u32[]{:S(2)}) collective-permute-start(f32[4,3,128]{2,1,0:T(4,128)S(1)} %pad_maximum_fusion), channel_id=1, source_target_pairs={{0,1},{1,0},{2,3},{3,2},{4,5},{5,4},{6,7},{7,6},{8,9},{9,8},{10,11... | collective-permute-start | bytes 18440 | tf_op jit(solution)/shard_map/ppermute | solution.py:18
  11.7 4.6 %collective-permute-start.6 = (f32[4,3,128]{2,1,0:T(4,128)S(1)}, f32[4,3,128]{2,1,0:T(4,128)S(1)}, u32[]{:S(2)}, u32[]{:S(2)}) collective-permute-start(f32[4,3,128]{2,1,0:T(4,128)S(1)} %fusion.12.after_ref), channel_id=1, source_target_pairs={{0,7},{1,6},{2,5},{3,4},{4,3},{5,2},{6,1},{7,0},{8,15},{9,14},{10,... | collective-permute-start | bytes 18440 | tf_op jit(solution)/shard_map/ppermute | solution.py:18
  14.3 3.1 %collective-permute-start.5 = (f32[4,3,128]{2,1,0:T(4,128)S(1)}, f32[4,3,128]{2,1,0:T(4,128)S(1)}, u32[]{:S(2)}, u32[]{:S(2)}) collective-permute-start(f32[4,3,128]{2,1,0:T(4,128)S(1)} %fusion.12.after_ref), channel_id=1, source_target_pairs={{0,5},{1,4},{2,7},{3,6},{4,1},{5,0},{6,3},{7,2},{8,13},{9,12},{10,... | collective-permute-start | bytes 18440 | tf_op jit(solution)/shard_map/ppermute | solution.py:18
  14.5 3.1 %collective-permute-start.4 = (f32[4,3,128]{2,1,0:T(4,128)S(1)}, f32[4,3,128]{2,1,0:T(4,128)S(1)}, u32[]{:S(2)}, u32[]{:S(2)}) collective-permute-start(f32[4,3,128]{2,1,0:T(4,128)S(1)} %fusion.12.after_ref), channel_id=1, source_target_pairs={{0,3},{1,2},{2,1},{3,0},{4,7},{5,6},{6,5},{7,4},{8,11},{9,10},{10,... | collective-permute-start | bytes 18440 | tf_op jit(solution)/shard_map/ppermute | solution.py:18
  16.3 1.4 %copy-start.1 = (bf16[128,512]{1,0:T(8,128)(2,1)S(1)}, bf16[128,512]{1,0:T(8,128)(2,1)}, u32[]{:S(2)}) copy-start(bf16[128,512]{1,0:T(8,128)(2,1)} %constant.18.clone.basis_ref) | copy-start | bytes 393220

commit v5 on v4

--- a/solution.py
+++ b/solution.py
@@ -174,35 +174,32 @@
     basis = jnp.asarray((rows * scale).astype(np.float32).astype(jnp.bfloat16))
 
 
-    got = swap(sent, "box", half ^ 1)
-    is_low = (me < half).astype(f32)
-    past = jnp.stack([got[0], sent[1]]) * is_low
-    total = jnp.stack([sym_total, got[1]])
-    state = jnp.concatenate([past, total])
-
     def later(mask):
         return ((me ^ mask) > me).astype(f32)
 
-    anti_part = got[2:]
-    got = swap(state, "box", 1)
-    sym_part = sym_part + later(1) * got[2]
-    anti_part = anti_part + later(1) * got[3]
-    state = state + got
+    total, anti_part = sent[:2], sent[2:]
+    got = swap(total, "box", 1)
+    sym_part = sym_part + later(1) * got[0]
+    anti_part = anti_part + (1.0 - later(1)) * got[1]
+    total = total + got
     spec, arm = pl.pallas_call(
         spectrum_kernel, out_shape=(pltpu.VMEM((gusts, wide), f32), pltpu.VMEM((2, s_dev, wide), f32)), name="spectrum"
-    )(gust_index.reshape(1, gusts), in_vmem(jnp.asarray(rows)), station_geom, in_vmem(state))
+    )(gust_index.reshape(1, gusts), in_vmem(jnp.asarray(rows)), station_geom, in_vmem(total))
     low, high = 1, half.bit_length() - 1
     while low < high:
         size = min(2, high - low)
         masks = [v << low for v in range(1, 1 << size)]
-        parts = [swap(state, "box", mask ^ 1) for mask in masks]
+        parts = [swap(total, "box", mask ^ 1) for mask in masks]
         for mask, part in zip(masks, parts):
-            sym_part = sym_part + later(mask) * part[2]
-            anti_part = anti_part + later(mask) * part[3]
-        state = state + sum(parts)
+            sym_part = sym_part + later(mask) * part[0]
+            anti_part = anti_part + later(mask) * part[1]
+        total = total + sum(parts)
         low += size
-    sym_part = sym_part + state[0]
-    anti_part = anti_part + state[1]
+    is_low = (me < half).astype(f32)
+    anti_part, spec, arm = lax.optimization_barrier((anti_part, spec, arm))
+    got = swap(jnp.concatenate([anti_part, total[:1]]), "box", half ^ 1)
+    anti_part = got[:-1] + is_low * total[1]
+    sym_part = sym_part + is_low * got[-1]
 
     out = pl.pallas_call(
         history_kernel,

time: 19.1 us -> 19 us (level)
  no operation moved by 1% of the time
where the time goes in v5:
time: 19 us; the launch traced here: 18.8 us
  starting transfers between devices  9.9 us (52%)
  Pallas kernels  4.89 us (26%)
  waiting for transfers between devices  3.87 us (20%)
    ppermute x7, starting transfers between devices, swap(): return lax.ppermute(block, axis, [(i, i ^ mask) for i in range(count)])  9.9 us
    ppermute x7, waiting for transfers between devices, swap(): return lax.ppermute(block, axis, [(i, i ^ mask) for i in range(count)])  3.87 us
    pallas_call x1, Pallas kernels, on_device(): pl.pallas_call(spectrum_kernel, out_shape=(pltpu.VMEM((gusts, wide), f32)...  1.58 us
    pallas_call x1, Pallas kernels, on_device(): pl.pallas_call(lambda *refs: sym_kernel(s_dev, *refs), out_shape=(pltpu.V...  1.19 us
    pallas_call x1, Pallas kernels, on_device(): pl.pallas_call(history_kernel, out_shape=jax.ShapeDtypeStruct((s_dev * 6...  1.17 us
    pallas_call x1, Pallas kernels, on_device(): pl.pallas_call(pack_kernel, out_shape=pltpu.VMEM((4, box_dev), f32), name...  0.71 us
  transfers between devices with their start and end apart: 7, of which 5 were waited for; matrix products, arithmetic and copies ran while one was open for 0% of the time, Pallas kernels for 19%

profile of v5, /device:TPU:0, one launch (start us, length us, event | category | flops | bytes accessed | tf_op | source)
XLA Modules:
  0.0 18.8 jit_solution(16640814838724987159)
XLA Ops:
  0.0 0.5 %collective-permute-start.1 = (f32[2,64,512]{2,1,0:T(8,128)}, f32[2,64,512]{2,1,0:T(8,128)S(1)}, u32[]{:S(2)}, u32[]{:S(2)}) collective-permute-start(f32[2,64,512]{2,1,0:T(8,128)} %param.9), channel_id=1, source_target_pairs={{0,1},{1,0},{2,3},{3,2},{4,5},{5,4},{6,7},{7,6},{8,9},{9,8},{10,11... | collective-permute-start | bytes 786440 | tf_op jit(solution)/shard_map/ppermute | solution.py:18
  0.5 0.7 %pack.1.refs_1_ = f32[4,512]{1,0:T(4,128)S(1)} custom-call(f32[3,512]{1,0:T(4,128)} %geom_ref.1, s32[4,128]{1,0:T(4,128)} %bitcast.23), custom_call_target="tpu_custom_call" | custom-call | tf_op jit(solution)/shard_map/pack/pallas_call | solution.py:158
  1.2 0.0 copy-start
  1.2 3.8 %collective-permute-start = (f32[4,512]{1,0:T(4,128)S(1)}, f32[4,512]{1,0:T(4,128)S(1)}, u32[]{:S(2)}, u32[]{:S(2)}) collective-permute-start(f32[4,512]{1,0:T(4,128)S(1)} %pack.1.refs_1_), channel_id=1, source_target_pairs={{0,9},{1,8},{2,11},{3,10},{4,13},{5,12},{6,15},{7,14},{8,1},{9,0},... | collective-permute-start | bytes 24584 | tf_op jit(solution)/shard_map/ppermute | solution.py:18
  4.9 1.2 %sym_sums.1 = (f32[3,128]{1,0:T(4,128)S(1)}, f32[2,3,128]{2,1,0:T(4,128)S(1)}) custom-call(f32[2,64,512]{2,1,0:T(8,128)} %refs_0_.1, f32[4,512]{1,0:T(4,128)S(1)} %pack.1.refs_1_), custom_call_target="tpu_custom_call" | custom-call | tf_op jit(solution)/shard_map/sym_sums/pallas_call | solution.py:161
  6.1 0.2 collective-permute-done.refs_0_
  6.3 0.0 collective-permute-done.1.refs_1_
  6.3 0.2 %anti_sums.1 = f32[4,3,128]{2,1,0:T(4,128)S(1)} custom-call(f32[4,512]{1,0:T(4,128)S(1)} %collective-permute-done.refs_0_, f32[2,64,512]{2,1,0:T(8,128)S(1)} %collective-permute-done.1.refs_1_, f32[3,128]{1,0:T(4,128)S(1)} %get-tuple-element.13.refs_2_), custom_call_target="tpu_custom_call" | custom-call | tf_op jit(solution)/shard_map/anti_sums/pallas_call | solution.py:166
  6.5 0.1 collective-permute-start.2
  6.6 1.1 %collective-permute-done.2 = f32[2,3,128]{2,1,0:T(4,128)S(1)} collective-permute-done((f32[2,3,128]{2,1,0:T(4,128)S(1)}, f32[2,3,128]{2,1,0:T(4,128)S(1)}, u32[]{:S(2)}, u32[]{:S(2)}) %collective-permute-start.2) | collective-permute-done | bytes 3104 | tf_op jit(solution)/shard_map/ppermute | solution.py:18
  7.7 2.6 %collective-permute-start.5 = (f32[2,3,128]{2,1,0:T(4,128)S(1)}, f32[2,3,128]{2,1,0:T(4,128)S(1)}, u32[]{:S(2)}, u32[]{:S(2)}) collective-permute-start(f32[2,3,128]{2,1,0:T(4,128)S(1)} %slice_add_fusion.2.after_ref), channel_id=1, source_target_pairs={{0,7},{1,6},{2,5},{3,4},{4,3},{5,2},{6,1},{7,0},{8,15},{9,14},{10,... | collective-permute-start | bytes 9224 | tf_op jit(solution)/shard_map/ppermute | solution.py:18
  10.3 0.2 %collective-permute-start.4 = (f32[2,3,128]{2,1,0:T(4,128)S(1)}, f32[2,3,128]{2,1,0:T(4,128)S(1)}, u32[]{:S(2)}, u32[]{:S(2)}) collective-permute-start(f32[2,3,128]{2,1,0:T(4,128)S(1)} %slice_add_fusion.2.after_ref), channel_id=1, source_target_pairs={{0,5},{1,4},{2,7},{3,6},{4,1},{5,0},{6,3},{7,2},{8,13},{9,12},{10,... | collective-permute-start | bytes 9224 | tf_op jit(solution)/shard_map/ppermute | solution.py:18
  10.5 0.2 %collective-permute-start.3 = (f32[2,3,128]{2,1,0:T(4,128)S(1)}, f32[2,3,128]{2,1,0:T(4,128)S(1)}, u32[]{:S(2)}, u32[]{:S(2)}) collective-permute-start(f32[2,3,128]{2,1,0:T(4,128)S(1)} %slice_add_fusion.2.after_ref), channel_id=1, source_target_pairs={{0,3},{1,2},{2,1},{3,0},{4,7},{5,6},{6,5},{7,4},{8,11},{9,10},{10,... | collective-permute-start | bytes 9224 | tf_op jit(solution)/shard_map/ppermute | solution.py:18
  10.7 0.0 copy-done
  10.7 1.6 %spectrum.1 = (f32[64,128]{1,0:T(8,128)S(1)}, f32[2,2,128]{2,1,0:T(2,128)S(1)}) custom-call(s32[1,64]{1,0:T(1,128)} %bitcast.24, f32[128,512]{1,0:T(8,128)S(1)} %copy-done, f32[2,2]{1,0:T(2,128)} %arm_ref.1, f32[2,3,128]{2,1,0:T(4,128)S(1)} %slice_add_fusion.2.after_ref), custom_call_target="tpu_custom_call" | custom-call | tf_op jit(solution)/shard_map/spectrum/pallas_call | solution.py:185
  12.3 0.0 copy-start.1
  12.3 0.0 collective-permute-done.5
  12.3 1.0 %collective-permute-done.4 = f32[2,3,128]{2,1,0:T(4,128)S(1)} collective-permute-done((f32[2,3,128]{2,1,0:T(4,128)S(1)}, f32[2,3,128]{2,1,0:T(4,128)S(1)}, u32[]{:S(2)}, u32[]{:S(2)}) %collective-permute-start.4) | collective-permute-done | bytes 3104 | tf_op jit(solution)/shard_map/ppermute | solution.py:18
  13.3 0.2 %collective-permute-done.3 = f32[2,3,128]{2,1,0:T(4,128)S(1)} collective-permute-done((f32[2,3,128]{2,1,0:T(4,128)S(1)}, f32[2,3,128]{2,1,0:T(4,128)S(1)}, u32[]{:S(2)}, u32[]{:S(2)}) %collective-permute-start.3) | collective-permute-done | bytes 3104 | tf_op jit(solution)/shard_map/ppermute | solution.py:18
  13.6 2.6 %collective-permute-start.6 = (f32[3,3,128]{2,1,0:T(4,128)S(1)}, f32[3,3,128]{2,1,0:T(4,128)S(1)}, u32[]{:S(2)}, u32[]{:S(2)}) collective-permute-start(f32[3,3,128]{2,1,0:T(4,128)S(1)} %pad_maximum_fusion), channel_id=1, source_target_pairs={{0,9},{1,8},{2,11},{3,10},{4,13},{5,12},{6,15},{7,14},{8,1},{9,0},... | collective-permute-start | bytes 13832 | tf_op jit(solution)/shard_map/ppermute | solution.py:18
  16.2 1.4 %collective-permute-done.6 = f32[3,3,128]{2,1,0:T(4,128)S(1)} collective-permute-done((f32[3,3,128]{2,1,0:T(4,128)S(1)}, f32[3,3,128]{2,1,0:T(4,128)S(1)}, u32[]{:S(2)}, u32[]{:S(2)}) %collective-permute-start.6) | collective-permute-done | bytes 4640 | tf_op jit(solution)/shard_map/ppermute | solution.py:18
  17.6 0.0 copy-done.1
  17.6 1.2 %histories.1 = bf16[768,512]{1,0:T(8,128)(2,1)} custom-call(f32[2,3,128]{2,1,0:T(4,128)S(1)} %get-tuple-element.30.sym_ref, f32[2,3,128]{2,1,0:T(4,128)S(1)} %get-tuple-element.29.anti_ref, f32[2,2,128]{2,1,0:T(2,128)S(1)} %get-tuple-element.17.arm_ref, f32[64,128]{1,0:T(8,128)S(1)} %get-tuple-element.18.spec_ref, bf16[128,512]{1,0:T(8,128)(2,1)S(1)} %copy-done.1), custom_call_target="tpu_custom_call" | custom-call | tf_op jit(solution)/shard_map/histories/pallas_call | solution.py:204
  (12 shorter events, 0.1 us)
Async XLA Ops:
  0.0 6.3 %collective-permute-start.1 = (f32[2,64,512]{2,1,0:T(8,128)}, f32[2,64,512]{2,1,0:T(8,128)S(1)}, u32[]{:S(2)}, u32[]{:S(2)}) collective-permute-start(f32[2,64,512]{2,1,0:T(8,128)} %param.9), channel_id=1, source_target_pairs={{0,1},{1,0},{2,3},{3,2},{4,5},{5,4},{6,7},{7,6},{8,9},{9,8},{10,11... | collective-permute-start | bytes 786440 | tf_op jit(solution)/shard_map/ppermute | solution.py:18
  1.2 9.6 %copy-start = (f32[128,512]{1,0:T(8,128)S(1)}, f32[128,512]{1,0:T(8,128)}, u32[]{:S(2)}) copy-start(f32[128,512]{1,0:T(8,128)} %constant.21.clone.rows_ref) | copy-start | bytes 786436
  1.2 5.1 %collective-permute-start = (f32[4,512]{1,0:T(4,128)S(1)}, f32[4,512]{1,0:T(4,128)S(1)}, u32[]{:S(2)}, u32[]{:S(2)}) collective-permute-start(f32[4,512]{1,0:T(4,128)S(1)} %pack.1.refs_1_), channel_id=1, source_target_pairs={{0,9},{1,8},{2,11},{3,10},{4,13},{5,12},{6,15},{7,14},{8,1},{9,0},... | collective-permute-start | bytes 24584 | tf_op jit(solution)/shard_map/ppermute | solution.py:18
  6.5 1.2 %collective-permute-start.2 = (f32[2,3,128]{2,1,0:T(4,128)S(1)}, f32[2,3,128]{2,1,0:T(4,128)S(1)}, u32[]{:S(2)}, u32[]{:S(2)}) collective-permute-start(f32[2,3,128]{2,1,0:T(4,128)S(1)} %slice.56), channel_id=1, source_target_pairs={{0,1},{1,0},{2,3},{3,2},{4,5},{5,4},{6,7},{7,6},{8,9},{9,8},{10,11... | collective-permute-start | bytes 9224 | tf_op jit(solution)/shard_map/ppermute | solution.py:18
  7.7 4.6 %collective-permute-start.5 = (f32[2,3,128]{2,1,0:T(4,128)S(1)}, f32[2,3,128]{2,1,0:T(4,128)S(1)}, u32[]{:S(2)}, u32[]{:S(2)}) collective-permute-start(f32[2,3,128]{2,1,0:T(4,128)S(1)} %slice_add_fusion.2.after_ref), channel_id=1, source_target_pairs={{0,7},{1,6},{2,5},{3,4},{4,3},{5,2},{6,1},{7,0},{8,15},{9,14},{10,... | collective-permute-start | bytes 9224 | tf_op jit(solution)/shard_map/ppermute | solution.py:18
  10.3 3.0 %collective-permute-start.4 = (f32[2,3,128]{2,1,0:T(4,128)S(1)}, f32[2,3,128]{2,1,0:T(4,128)S(1)}, u32[]{:S(2)}, u32[]{:S(2)}) collective-permute-start(f32[2,3,128]{2,1,0:T(4,128)S(1)} %slice_add_fusion.2.after_ref), channel_id=1, source_target_pairs={{0,5},{1,4},{2,7},{3,6},{4,1},{5,0},{6,3},{7,2},{8,13},{9,12},{10,... | collective-permute-start | bytes 9224 | tf_op jit(solution)/shard_map/ppermute | solution.py:18
  10.5 3.0 %collective-permute-start.3 = (f32[2,3,128]{2,1,0:T(4,128)S(1)}, f32[2,3,128]{2,1,0:T(4,128)S(1)}, u32[]{:S(2)}, u32[]{:S(2)}) collective-permute-start(f32[2,3,128]{2,1,0:T(4,128)S(1)} %slice_add_fusion.2.after_ref), channel_id=1, source_target_pairs={{0,3},{1,2},{2,1},{3,0},{4,7},{5,6},{6,5},{7,4},{8,11},{9,10},{10,... | collective-permute-start | bytes 9224 | tf_op jit(solution)/shard_map/ppermute | solution.py:18
  12.3 5.3 %copy-start.1 = (bf16[128,512]{1,0:T(8,128)(2,1)S(1)}, bf16[128,512]{1,0:T(8,128)(2,1)}, u32[]{:S(2)}) copy-start(bf16[128,512]{1,0:T(8,128)(2,1)} %constant.20.clone.basis_ref) | copy-start | bytes 393220
  13.6 4.0 %collective-permute-start.6 = (f32[3,3,128]{2,1,0:T(4,128)S(1)}, f32[3,3,128]{2,1,0:T(4,128)S(1)}, u32[]{:S(2)}, u32[]{:S(2)}) collective-permute-start(f32[3,3,128]{2,1,0:T(4,128)S(1)} %pad_maximum_fusion), channel_id=1, source_target_pairs={{0,9},{1,8},{2,11},{3,10},{4,13},{5,12},{6,15},{7,14},{8,1},{9,0},... | collective-permute-start | bytes 13832 | tf_op jit(solution)/shard_map/ppermute | solution.py:18

commit v6 on v5

--- a/solution.py
+++ b/solution.py
@@ -46,18 +46,6 @@
     last = row[:, row.shape[1] - 1 :]
     passed = jnp.broadcast_to(row - last, step.shape) >= step - s_dev
     return jnp.where((step == 0) | passed, 1.0, 0.0).astype(jnp.bfloat16)
-
-
-def pack_kernel(geom_ref, ids_ref, out_ref):
-    ids = ids_ref[...].astype(jnp.float32)
-    out_ref[0:3] = geom_ref[...]
-    out_ref[3:4] = jnp.concatenate([ids[i : i + 1] for i in range(ids.shape[0])], 1)
-
-
-def pack_kernel(geom_ref, ids_ref, out_ref):
-    ids = ids_ref[...].astype(jnp.float32)
-    out_ref[0:3] = geom_ref[...]
-    out_ref[3:4] = jnp.concatenate([ids[i : i + 1] for i in range(ids.shape[0])], 1)
 
 
 def pack_kernel(geom_ref, ids_ref, out_ref):
@@ -172,7 +160,6 @@
     rows = fourier_rows(freqs, NFFT)
     scale = np.where(np.arange(wide) % freqs == 0, 1.0, 2.0)[:, None] / NFFT
     basis = jnp.asarray((rows * scale).astype(np.float32).astype(jnp.bfloat16))
-
 
     def later(mask):
         return ((me ^ mask) > me).astype(f32)

time: 19 us -> 19 us (level)
  no operation moved by 1% of the time
where the time goes in v6:
time: 19 us; the launch traced here: 18.8 us
  starting transfers between devices  9.9 us (52%)
  Pallas kernels  4.89 us (26%)
  waiting for transfers between devices  3.87 us (20%)
    ppermute x7, starting transfers between devices, swap(): return lax.ppermute(block, axis, [(i, i ^ mask) for i in range(count)])  9.9 us
    ppermute x7, waiting for transfers between devices, swap(): return lax.ppermute(block, axis, [(i, i ^ mask) for i in range(count)])  3.87 us
    pallas_call x1, Pallas kernels, on_device(): pl.pallas_call(spectrum_kernel, out_shape=(pltpu.VMEM((gusts, wide), f32)...  1.58 us
    pallas_call x1, Pallas kernels, on_device(): pl.pallas_call(lambda *refs: sym_kernel(s_dev, *refs), out_shape=(pltpu.V...  1.19 us
    pallas_call x1, Pallas kernels, on_device(): pl.pallas_call(history_kernel, out_shape=jax.ShapeDtypeStruct((s_dev * 6...  1.17 us
    pallas_call x1, Pallas kernels, on_device(): pl.pallas_call(pack_kernel, out_shape=pltpu.VMEM((4, box_dev), f32), name...  0.71 us
  transfers between devices with their start and end apart: 7, of which 5 were waited for; matrix products, arithmetic and copies ran while one was open for 0% of the time, Pallas kernels for 19%

profile of v6, /device:TPU:0, one launch (start us, length us, event | category | flops | bytes accessed | tf_op | source)
XLA Modules:
  0.0 18.8 jit_solution(16640814838724987159)
XLA Ops:
  0.0 0.5 %collective-permute-start.1 = (f32[2,64,512]{2,1,0:T(8,128)}, f32[2,64,512]{2,1,0:T(8,128)S(1)}, u32[]{:S(2)}, u32[]{:S(2)}) collective-permute-start(f32[2,64,512]{2,1,0:T(8,128)} %param.9), channel_id=1, source_target_pairs={{0,1},{1,0},{2,3},{3,2},{4,5},{5,4},{6,7},{7,6},{8,9},{9,8},{10,11... | collective-permute-start | bytes 786440 | tf_op jit(solution)/shard_map/ppermute | solution.py:18
  0.5 0.7 %pack.1.refs_1_ = f32[4,512]{1,0:T(4,128)S(1)} custom-call(f32[3,512]{1,0:T(4,128)} %geom_ref.1, s32[4,128]{1,0:T(4,128)} %bitcast.23), custom_call_target="tpu_custom_call" | custom-call | tf_op jit(solution)/shard_map/pack/pallas_call | solution.py:146
  1.2 0.0 copy-start
  1.2 3.8 %collective-permute-start = (f32[4,512]{1,0:T(4,128)S(1)}, f32[4,512]{1,0:T(4,128)S(1)}, u32[]{:S(2)}, u32[]{:S(2)}) collective-permute-start(f32[4,512]{1,0:T(4,128)S(1)} %pack.1.refs_1_), channel_id=1, source_target_pairs={{0,9},{1,8},{2,11},{3,10},{4,13},{5,12},{6,15},{7,14},{8,1},{9,0},... | collective-permute-start | bytes 24584 | tf_op jit(solution)/shard_map/ppermute | solution.py:18
  4.9 1.2 %sym_sums.1 = (f32[3,128]{1,0:T(4,128)S(1)}, f32[2,3,128]{2,1,0:T(4,128)S(1)}) custom-call(f32[2,64,512]{2,1,0:T(8,128)} %refs_0_.1, f32[4,512]{1,0:T(4,128)S(1)} %pack.1.refs_1_), custom_call_target="tpu_custom_call" | custom-call | tf_op jit(solution)/shard_map/sym_sums/pallas_call | solution.py:149
  6.1 0.2 collective-permute-done.refs_0_
  6.3 0.0 collective-permute-done.1.refs_1_
  6.3 0.2 %anti_sums.1 = f32[4,3,128]{2,1,0:T(4,128)S(1)} custom-call(f32[4,512]{1,0:T(4,128)S(1)} %collective-permute-done.refs_0_, f32[2,64,512]{2,1,0:T(8,128)S(1)} %collective-permute-done.1.refs_1_, f32[3,128]{1,0:T(4,128)S(1)} %get-tuple-element.13.refs_2_), custom_call_target="tpu_custom_call" | custom-call | tf_op jit(solution)/shard_map/anti_sums/pallas_call | solution.py:154
  6.5 0.1 collective-permute-start.2
  6.6 1.1 %collective-permute-done.2 = f32[2,3,128]{2,1,0:T(4,128)S(1)} collective-permute-done((f32[2,3,128]{2,1,0:T(4,128)S(1)}, f32[2,3,128]{2,1,0:T(4,128)S(1)}, u32[]{:S(2)}, u32[]{:S(2)}) %collective-permute-start.2) | collective-permute-done | bytes 3104 | tf_op jit(solution)/shard_map/ppermute | solution.py:18
  7.7 2.6 %collective-permute-start.5 = (f32[2,3,128]{2,1,0:T(4,128)S(1)}, f32[2,3,128]{2,1,0:T(4,128)S(1)}, u32[]{:S(2)}, u32[]{:S(2)}) collective-permute-start(f32[2,3,128]{2,1,0:T(4,128)S(1)} %slice_add_fusion.2.after_ref), channel_id=1, source_target_pairs={{0,7},{1,6},{2,5},{3,4},{4,3},{5,2},{6,1},{7,0},{8,15},{9,14},{10,... | collective-permute-start | bytes 9224 | tf_op jit(solution)/shard_map/ppermute | solution.py:18
  10.3 0.2 %collective-permute-start.4 = (f32[2,3,128]{2,1,0:T(4,128)S(1)}, f32[2,3,128]{2,1,0:T(4,128)S(1)}, u32[]{:S(2)}, u32[]{:S(2)}) collective-permute-start(f32[2,3,128]{2,1,0:T(4,128)S(1)} %slice_add_fusion.2.after_ref), channel_id=1, source_target_pairs={{0,5},{1,4},{2,7},{3,6},{4,1},{5,0},{6,3},{7,2},{8,13},{9,12},{10,... | collective-permute-start | bytes 9224 | tf_op jit(solution)/shard_map/ppermute | solution.py:18
  10.5 0.2 %collective-permute-start.3 = (f32[2,3,128]{2,1,0:T(4,128)S(1)}, f32[2,3,128]{2,1,0:T(4,128)S(1)}, u32[]{:S(2)}, u32[]{:S(2)}) collective-permute-start(f32[2,3,128]{2,1,0:T(4,128)S(1)} %slice_add_fusion.2.after_ref), channel_id=1, source_target_pairs={{0,3},{1,2},{2,1},{3,0},{4,7},{5,6},{6,5},{7,4},{8,11},{9,10},{10,... | collective-permute-start | bytes 9224 | tf_op jit(solution)/shard_map/ppermute | solution.py:18
  10.7 0.0 copy-done
  10.7 1.6 %spectrum.1 = (f32[64,128]{1,0:T(8,128)S(1)}, f32[2,2,128]{2,1,0:T(2,128)S(1)}) custom-call(s32[1,64]{1,0:T(1,128)} %bitcast.24, f32[128,512]{1,0:T(8,128)S(1)} %copy-done, f32[2,2]{1,0:T(2,128)} %arm_ref.1, f32[2,3,128]{2,1,0:T(4,128)S(1)} %slice_add_fusion.2.after_ref), custom_call_target="tpu_custom_call" | custom-call | tf_op jit(solution)/shard_map/spectrum/pallas_call | solution.py:172
  12.3 0.0 copy-start.1
  12.3 0.0 collective-permute-done.5
  12.3 1.0 %collective-permute-done.4 = f32[2,3,128]{2,1,0:T(4,128)S(1)} collective-permute-done((f32[2,3,128]{2,1,0:T(4,128)S(1)}, f32[2,3,128]{2,1,0:T(4,128)S(1)}, u32[]{:S(2)}, u32[]{:S(2)}) %collective-permute-start.4) | collective-permute-done | bytes 3104 | tf_op jit(solution)/shard_map/ppermute | solution.py:18
  13.3 0.2 %collective-permute-done.3 = f32[2,3,128]{2,1,0:T(4,128)S(1)} collective-permute-done((f32[2,3,128]{2,1,0:T(4,128)S(1)}, f32[2,3,128]{2,1,0:T(4,128)S(1)}, u32[]{:S(2)}, u32[]{:S(2)}) %collective-permute-start.3) | collective-permute-done | bytes 3104 | tf_op jit(solution)/shard_map/ppermute | solution.py:18
  13.6 2.6 %collective-permute-start.6 = (f32[3,3,128]{2,1,0:T(4,128)S(1)}, f32[3,3,128]{2,1,0:T(4,128)S(1)}, u32[]{:S(2)}, u32[]{:S(2)}) collective-permute-start(f32[3,3,128]{2,1,0:T(4,128)S(1)} %pad_maximum_fusion), channel_id=1, source_target_pairs={{0,9},{1,8},{2,11},{3,10},{4,13},{5,12},{6,15},{7,14},{8,1},{9,0},... | collective-permute-start | bytes 13832 | tf_op jit(solution)/shard_map/ppermute | solution.py:18
  16.2 1.4 %collective-permute-done.6 = f32[3,3,128]{2,1,0:T(4,128)S(1)} collective-permute-done((f32[3,3,128]{2,1,0:T(4,128)S(1)}, f32[3,3,128]{2,1,0:T(4,128)S(1)}, u32[]{:S(2)}, u32[]{:S(2)}) %collective-permute-start.6) | collective-permute-done | bytes 4640 | tf_op jit(solution)/shard_map/ppermute | solution.py:18
  17.6 0.0 copy-done.1
  17.6 1.2 %histories.1 = bf16[768,512]{1,0:T(8,128)(2,1)} custom-call(f32[2,3,128]{2,1,0:T(4,128)S(1)} %get-tuple-element.30.sym_ref, f32[2,3,128]{2,1,0:T(4,128)S(1)} %get-tuple-element.29.anti_ref, f32[2,2,128]{2,1,0:T(2,128)S(1)} %get-tuple-element.17.arm_ref, f32[64,128]{1,0:T(8,128)S(1)} %get-tuple-element.18.spec_ref, bf16[128,512]{1,0:T(8,128)(2,1)S(1)} %copy-done.1), custom_call_target="tpu_custom_call" | custom-call | tf_op jit(solution)/shard_map/histories/pallas_call | solution.py:191
  (12 shorter events, 0.1 us)
Async XLA Ops:
  0.0 6.3 %collective-permute-start.1 = (f32[2,64,512]{2,1,0:T(8,128)}, f32[2,64,512]{2,1,0:T(8,128)S(1)}, u32[]{:S(2)}, u32[]{:S(2)}) collective-permute-start(f32[2,64,512]{2,1,0:T(8,128)} %param.9), channel_id=1, source_target_pairs={{0,1},{1,0},{2,3},{3,2},{4,5},{5,4},{6,7},{7,6},{8,9},{9,8},{10,11... | collective-permute-start | bytes 786440 | tf_op jit(solution)/shard_map/ppermute | solution.py:18
  1.2 9.6 %copy-start = (f32[128,512]{1,0:T(8,128)S(1)}, f32[128,512]{1,0:T(8,128)}, u32[]{:S(2)}) copy-start(f32[128,512]{1,0:T(8,128)} %constant.21.clone.rows_ref) | copy-start | bytes 786436
  1.2 5.1 %collective-permute-start = (f32[4,512]{1,0:T(4,128)S(1)}, f32[4,512]{1,0:T(4,128)S(1)}, u32[]{:S(2)}, u32[]{:S(2)}) collective-permute-start(f32[4,512]{1,0:T(4,128)S(1)} %pack.1.refs_1_), channel_id=1, source_target_pairs={{0,9},{1,8},{2,11},{3,10},{4,13},{5,12},{6,15},{7,14},{8,1},{9,0},... | collective-permute-start | bytes 24584 | tf_op jit(solution)/shard_map/ppermute | solution.py:18
  6.5 1.2 %collective-permute-start.2 = (f32[2,3,128]{2,1,0:T(4,128)S(1)}, f32[2,3,128]{2,1,0:T(4,128)S(1)}, u32[]{:S(2)}, u32[]{:S(2)}) collective-permute-start(f32[2,3,128]{2,1,0:T(4,128)S(1)} %slice.56), channel_id=1, source_target_pairs={{0,1},{1,0},{2,3},{3,2},{4,5},{5,4},{6,7},{7,6},{8,9},{9,8},{10,11... | collective-permute-start | bytes 9224 | tf_op jit(solution)/shard_map/ppermute | solution.py:18
  7.7 4.6 %collective-permute-start.5 = (f32[2,3,128]{2,1,0:T(4,128)S(1)}, f32[2,3,128]{2,1,0:T(4,128)S(1)}, u32[]{:S(2)}, u32[]{:S(2)}) collective-permute-start(f32[2,3,128]{2,1,0:T(4,128)S(1)} %slice_add_fusion.2.after_ref), channel_id=1, source_target_pairs={{0,7},{1,6},{2,5},{3,4},{4,3},{5,2},{6,1},{7,0},{8,15},{9,14},{10,... | collective-permute-start | bytes 9224 | tf_op jit(solution)/shard_map/ppermute | solution.py:18
  10.3 3.0 %collective-permute-start.4 = (f32[2,3,128]{2,1,0:T(4,128)S(1)}, f32[2,3,128]{2,1,0:T(4,128)S(1)}, u32[]{:S(2)}, u32[]{:S(2)}) collective-permute-start(f32[2,3,128]{2,1,0:T(4,128)S(1)} %slice_add_fusion.2.after_ref), channel_id=1, source_target_pairs={{0,5},{1,4},{2,7},{3,6},{4,1},{5,0},{6,3},{7,2},{8,13},{9,12},{10,... | collective-permute-start | bytes 9224 | tf_op jit(solution)/shard_map/ppermute | solution.py:18
  10.5 3.0 %collective-permute-start.3 = (f32[2,3,128]{2,1,0:T(4,128)S(1)}, f32[2,3,128]{2,1,0:T(4,128)S(1)}, u32[]{:S(2)}, u32[]{:S(2)}) collective-permute-start(f32[2,3,128]{2,1,0:T(4,128)S(1)} %slice_add_fusion.2.after_ref), channel_id=1, source_target_pairs={{0,3},{1,2},{2,1},{3,0},{4,7},{5,6},{6,5},{7,4},{8,11},{9,10},{10,... | collective-permute-start | bytes 9224 | tf_op jit(solution)/shard_map/ppermute | solution.py:18
  12.3 5.3 %copy-start.1 = (bf16[128,512]{1,0:T(8,128)(2,1)S(1)}, bf16[128,512]{1,0:T(8,128)(2,1)}, u32[]{:S(2)}) copy-start(bf16[128,512]{1,0:T(8,128)(2,1)} %constant.20.clone.basis_ref) | copy-start | bytes 393220
  13.6 4.0 %collective-permute-start.6 = (f32[3,3,128]{2,1,0:T(4,128)S(1)}, f32[3,3,128]{2,1,0:T(4,128)S(1)}, u32[]{:S(2)}, u32[]{:S(2)}) collective-permute-start(f32[3,3,128]{2,1,0:T(4,128)S(1)} %pad_maximum_fusion), channel_id=1, source_target_pairs={{0,9},{1,8},{2,11},{3,10},{4,13},{5,12},{6,15},{7,14},{8,1},{9,0},... | collective-permute-start | bytes 13832 | tf_op jit(solution)/shard_map/ppermute | solution.py:18

commit v7 on v6

--- a/solution.py
+++ b/solution.py
@@ -64,14 +64,21 @@
             part_ref[k, moment : moment + 1] = sums[moment][1 + k : 2 + k]
 
 
-def anti_kernel(s_dev, geom_ref, anti_ref, sym_ref, sent_ref):
+def anti_total_kernel(geom_ref, anti_ref, sym_ref, sent_ref):
+    rows = 2 * anti_ref.shape[1]
+    sums = block_sums(anti_ref[...].reshape(rows, -1), geom_ref[...], jnp.ones((8, geom_ref.shape[1]), jnp.bfloat16))
+    sent_ref[0] = sym_ref[...]
+    for moment in range(3):
+        sent_ref[1, moment : moment + 1] = sums[moment][0:1]
+
+
+def anti_part_kernel(s_dev, geom_ref, anti_ref, after_ref, part_ref):
     geom = geom_ref[...]
     rows = 2 * anti_ref.shape[1]
     sums = block_sums(anti_ref[...].reshape(rows, -1), geom, station_marks(geom[3:4], s_dev))
-    sent_ref[0] = sym_ref[...]
-    for moment in range(3):
-        for k in range(1 + s_dev):
-            sent_ref[1 + k, moment : moment + 1] = sums[moment][k : k + 1]
+    for moment in range(3):
+        for k in range(s_dev):
+            part_ref[k, moment : moment + 1] = sums[moment][1 + k : 2 + k]
 
 
 def spectrum_kernel(index_ref, rows_ref, arm_ref, after_ref, spec_ref, arms_ref):
@@ -151,10 +158,8 @@
         out_shape=(pltpu.VMEM((3, wide), f32), pltpu.VMEM((s_dev, 3, wide), f32)),
         name="sym_sums",
     )(sym_press, in_vmem(geom))
-    sent = pl.pallas_call(
-        lambda *refs: anti_kernel(s_dev, *refs),
-        out_shape=pltpu.VMEM((2 + s_dev, 3, wide), f32),
-        name="anti_sums",
+    total = pl.pallas_call(
+        anti_total_kernel, out_shape=pltpu.VMEM((2, 3, wide), f32), name="anti_totals"
     )(in_vmem(far_geom), in_vmem(near_anti), in_vmem(sym_total))
 
     rows = fourier_rows(freqs, NFFT)
@@ -164,11 +169,15 @@
     def later(mask):
         return ((me ^ mask) > me).astype(f32)
 
-    total, anti_part = sent[:2], sent[2:]
     got = swap(total, "box", 1)
     sym_part = sym_part + later(1) * got[0]
-    anti_part = anti_part + (1.0 - later(1)) * got[1]
+    anti_past = (1.0 - later(1)) * got[1]
     total = total + got
+    anti_part = pl.pallas_call(
+        lambda *refs: anti_part_kernel(s_dev, *refs),
+        out_shape=pltpu.VMEM((s_dev, 3, wide), f32),
+        name="anti_parts",
+    )(in_vmem(far_geom), in_vmem(near_anti), in_vmem(total))
     spec, arm = pl.pallas_call(
         spectrum_kernel, out_shape=(pltpu.VMEM((gusts, wide), f32), pltpu.VMEM((2, s_dev, wide), f32)), name="spectrum"
     )(gust_index.reshape(1, gusts), in_vmem(jnp.asarray(rows)), station_geom, in_vmem(total))
@@ -179,12 +188,12 @@
         parts = [swap(total, "box", mask ^ 1) for mask in masks]
         for mask, part in zip(masks, parts):
             sym_part = sym_part + later(mask) * part[0]
-            anti_part = anti_part + later(mask) * part[1]
+            anti_past = anti_past + later(mask) * part[1]
         total = total + sum(parts)
         low += size
     is_low = (me < half).astype(f32)
     anti_part, spec, arm = lax.optimization_barrier((anti_part, spec, arm))
-    got = swap(jnp.concatenate([anti_part, total[:1]]), "box", half ^ 1)
+    got = swap(jnp.concatenate([anti_part + anti_past, total[:1]]), "box", half ^ 1)
     anti_part = got[:-1] + is_low * total[1]
     sym_part = sym_part + is_low * got[-1]
 

time: 19 us -> 19 us (level)
  waiting for transfers between devices: 3.87 us -> 3.66 us
  Pallas kernels: 4.89 us -> 5.09 us
    pallas_call x1 -> x2, Pallas kernels: 0.24 us -> 0.45 us  [the longest x1 0.24 us: on_device(): pl.pallas_call(lambda *refs: anti_part_kernel(s_dev, *refs), out_shape=pl...]
    ppermute x7, waiting for transfers between devices: 3.87 us -> 3.66 us  [swap(): return lax.ppermute(block, axis, [(i, i ^ mask) for i in range(count)])]
  transfers between devices with their start and end apart: 7 -> 7, of which waited for: 5 -> 5; matrix products, arithmetic and copies ran while one was open for 0% -> 0% of each run, Pallas kernels for 19% -> 20%
where the time goes in v7:
time: 19 us; the launch traced here: 18.8 us
  starting transfers between devices  9.9 us (52%)
  Pallas kernels  5.09 us (27%)
  waiting for transfers between devices  3.66 us (19%)
    ppermute x7, starting transfers between devices, swap(): return lax.ppermute(block, axis, [(i, i ^ mask) for i in range(count)])  9.9 us
    ppermute x7, waiting for transfers between devices, swap(): return lax.ppermute(block, axis, [(i, i ^ mask) for i in range(count)])  3.66 us
    pallas_call x1, Pallas kernels, on_device(): pl.pallas_call(spectrum_kernel, out_shape=(pltpu.VMEM((gusts, wide), f32)...  1.58 us
    pallas_call x1, Pallas kernels, on_device(): pl.pallas_call(lambda *refs: sym_kernel(s_dev, *refs), out_shape=(pltpu.V...  1.19 us
    pallas_call x1, Pallas kernels, on_device(): pl.pallas_call(history_kernel, out_shape=jax.ShapeDtypeStruct((s_dev * 6...  1.17 us
    pallas_call x1, Pallas kernels, on_device(): pl.pallas_call(pack_kernel, out_shape=pltpu.VMEM((4, box_dev), f32), name...  0.71 us
  transfers between devices with their start and end apart: 7, of which 5 were waited for; matrix products, arithmetic and copies ran while one was open for 0% of the time, Pallas kernels for 20%

profile of v7, /device:TPU:0, one launch (start us, length us, event | category | flops | bytes accessed | tf_op | source)
XLA Modules:
  0.0 18.8 jit_solution(9844390531117475212)
XLA Ops:
  0.0 0.5 %collective-permute-start.1 = (f32[2,64,512]{2,1,0:T(8,128)}, f32[2,64,512]{2,1,0:T(8,128)S(1)}, u32[]{:S(2)}, u32[]{:S(2)}) collective-permute-start(f32[2,64,512]{2,1,0:T(8,128)} %param.9), channel_id=1, source_target_pairs={{0,1},{1,0},{2,3},{3,2},{4,5},{5,4},{6,7},{7,6},{8,9},{9,8},{10,11... | collective-permute-start | bytes 786440 | tf_op jit(solution)/shard_map/ppermute | solution.py:18
  0.5 0.7 %pack.1.refs_1_ = f32[4,512]{1,0:T(4,128)S(1)} custom-call(f32[3,512]{1,0:T(4,128)} %geom_ref.1, s32[4,128]{1,0:T(4,128)} %bitcast.17), custom_call_target="tpu_custom_call" | custom-call | tf_op jit(solution)/shard_map/pack/pallas_call | solution.py:153
  1.2 0.0 copy-start
  1.2 3.8 %collective-permute-start = (f32[4,512]{1,0:T(4,128)S(1)}, f32[4,512]{1,0:T(4,128)S(1)}, u32[]{:S(2)}, u32[]{:S(2)}) collective-permute-start(f32[4,512]{1,0:T(4,128)S(1)} %pack.1.refs_1_), channel_id=1, source_target_pairs={{0,9},{1,8},{2,11},{3,10},{4,13},{5,12},{6,15},{7,14},{8,1},{9,0},... | collective-permute-start | bytes 24584 | tf_op jit(solution)/shard_map/ppermute | solution.py:18
  4.9 1.2 %sym_sums.1 = (f32[3,128]{1,0:T(4,128)S(1)}, f32[2,3,128]{2,1,0:T(4,128)S(1)}) custom-call(f32[2,64,512]{2,1,0:T(8,128)} %refs_0_.1, f32[4,512]{1,0:T(4,128)S(1)} %pack.1.refs_1_), custom_call_target="tpu_custom_call" | custom-call | tf_op jit(solution)/shard_map/sym_sums/pallas_call | solution.py:156
  6.1 0.2 collective-permute-done.geom_ref.refs_0_
  6.3 0.0 collective-permute-done.1.anti_ref.refs_1_
  6.3 0.2 %anti_totals.1 = f32[2,3,128]{2,1,0:T(4,128)S(1)} custom-call(f32[4,512]{1,0:T(4,128)S(1)} %collective-permute-done.geom_ref.refs_0_, f32[2,64,512]{2,1,0:T(8,128)S(1)} %collective-permute-done.1.anti_ref.refs_1_, f32[3,128]{1,0:T(4,128)S(1)} %get-tuple-element.13.sym_ref), custom_call_target="tpu_custom_call" | custom-call | tf_op jit(solution)/shard_map/anti_totals/pallas_call | solution.py:161
  6.5 0.1 collective-permute-start.2
  6.6 1.1 %collective-permute-done.2 = f32[2,3,128]{2,1,0:T(4,128)S(1)} collective-permute-done((f32[2,3,128]{2,1,0:T(4,128)S(1)}, f32[2,3,128]{2,1,0:T(4,128)S(1)}, u32[]{:S(2)}, u32[]{:S(2)}) %collective-permute-start.2) | collective-permute-done | bytes 3104 | tf_op jit(solution)/shard_map/ppermute | solution.py:18
  7.7 2.6 %collective-permute-start.5 = (f32[2,3,128]{2,1,0:T(4,128)S(1)}, f32[2,3,128]{2,1,0:T(4,128)S(1)}, u32[]{:S(2)}, u32[]{:S(2)}) collective-permute-start(f32[2,3,128]{2,1,0:T(4,128)S(1)} %add.97.refs_2_.after_ref), channel_id=1, source_target_pairs={{0,7},{1,6},{2,5},{3,4},{4,3},{5,2},{6,1},{7,0},{8,15},{9,14},{10,... | collective-permute-start | bytes 9224 | tf_op jit(solution)/shard_map/ppermute | solution.py:18
  10.2 0.2 %collective-permute-start.4 = (f32[2,3,128]{2,1,0:T(4,128)S(1)}, f32[2,3,128]{2,1,0:T(4,128)S(1)}, u32[]{:S(2)}, u32[]{:S(2)}) collective-permute-start(f32[2,3,128]{2,1,0:T(4,128)S(1)} %add.97.refs_2_.after_ref), channel_id=1, source_target_pairs={{0,5},{1,4},{2,7},{3,6},{4,1},{5,0},{6,3},{7,2},{8,13},{9,12},{10,... | collective-permute-start | bytes 9224 | tf_op jit(solution)/shard_map/ppermute | solution.py:18
  10.5 0.2 %collective-permute-start.3 = (f32[2,3,128]{2,1,0:T(4,128)S(1)}, f32[2,3,128]{2,1,0:T(4,128)S(1)}, u32[]{:S(2)}, u32[]{:S(2)}) collective-permute-start(f32[2,3,128]{2,1,0:T(4,128)S(1)} %add.97.refs_2_.after_ref), channel_id=1, source_target_pairs={{0,3},{1,2},{2,1},{3,0},{4,7},{5,6},{6,5},{7,4},{8,11},{9,10},{10,... | collective-permute-start | bytes 9224 | tf_op jit(solution)/shard_map/ppermute | solution.py:18
  10.7 0.0 copy-done
  10.7 1.6 %spectrum.1 = (f32[64,128]{1,0:T(8,128)S(1)}, f32[2,2,128]{2,1,0:T(2,128)S(1)}) custom-call(s32[1,64]{1,0:T(1,128)} %bitcast.18, f32[128,512]{1,0:T(8,128)S(1)} %copy-done, f32[2,2]{1,0:T(2,128)} %arm_ref.1, f32[2,3,128]{2,1,0:T(4,128)S(1)} %add.97.refs_2_.after_ref), custom_call_target="tpu_custom_call" | custom-call | tf_op jit(solution)/shard_map/spectrum/pallas_call | solution.py:181
  12.3 0.2 %anti_parts.1 = f32[2,3,128]{2,1,0:T(4,128)S(1)} custom-call(f32[4,512]{1,0:T(4,128)S(1)} %collective-permute-done.geom_ref.refs_0_, f32[2,64,512]{2,1,0:T(8,128)S(1)} %collective-permute-done.1.anti_ref.refs_1_, f32[2,3,128]{2,1,0:T(4,128)S(1)} %add.97.refs_2_.after_ref), custom_call_target="tpu_custom_call" | custom-call | tf_op jit(solution)/shard_map/anti_parts/pallas_call | solution.py:176
  12.5 0.0 copy-start.1
  12.5 0.0 collective-permute-done.5
  12.5 0.8 %collective-permute-done.4 = f32[2,3,128]{2,1,0:T(4,128)S(1)} collective-permute-done((f32[2,3,128]{2,1,0:T(4,128)S(1)}, f32[2,3,128]{2,1,0:T(4,128)S(1)}, u32[]{:S(2)}, u32[]{:S(2)}) %collective-permute-start.4) | collective-permute-done | bytes 3104 | tf_op jit(solution)/shard_map/ppermute | solution.py:18
  13.3 0.2 %collective-permute-done.3 = f32[2,3,128]{2,1,0:T(4,128)S(1)} collective-permute-done((f32[2,3,128]{2,1,0:T(4,128)S(1)}, f32[2,3,128]{2,1,0:T(4,128)S(1)}, u32[]{:S(2)}, u32[]{:S(2)}) %collective-permute-start.3) | collective-permute-done | bytes 3104 | tf_op jit(solution)/shard_map/ppermute | solution.py:18
  13.6 2.6 %collective-permute-start.6 = (f32[3,3,128]{2,1,0:T(4,128)S(1)}, f32[3,3,128]{2,1,0:T(4,128)S(1)}, u32[]{:S(2)}, u32[]{:S(2)}) collective-permute-start(f32[3,3,128]{2,1,0:T(4,128)S(1)} %pad_maximum_fusion), channel_id=1, source_target_pairs={{0,9},{1,8},{2,11},{3,10},{4,13},{5,12},{6,15},{7,14},{8,1},{9,0},... | collective-permute-start | bytes 13832 | tf_op jit(solution)/shard_map/ppermute | solution.py:18
  16.2 1.4 %collective-permute-done.6 = f32[3,3,128]{2,1,0:T(4,128)S(1)} collective-permute-done((f32[3,3,128]{2,1,0:T(4,128)S(1)}, f32[3,3,128]{2,1,0:T(4,128)S(1)}, u32[]{:S(2)}, u32[]{:S(2)}) %collective-permute-start.6) | collective-permute-done | bytes 4640 | tf_op jit(solution)/shard_map/ppermute | solution.py:18
  17.6 0.0 copy-done.1
  17.6 1.2 %histories.1 = bf16[768,512]{1,0:T(8,128)(2,1)} custom-call(f32[2,3,128]{2,1,0:T(4,128)S(1)} %get-tuple-element.27.sym_ref, f32[2,3,128]{2,1,0:T(4,128)S(1)} %get-tuple-element.26.anti_ref, f32[2,2,128]{2,1,0:T(2,128)S(1)} %get-tuple-element.17.arm_ref, f32[64,128]{1,0:T(8,128)S(1)} %get-tuple-element.18.spec_ref, bf16[128,512]{1,0:T(8,128)(2,1)S(1)} %copy-done.1), custom_call_target="tpu_custom_call" | custom-call | tf_op jit(solution)/shard_map/histories/pallas_call | solution.py:200
  (8 shorter events, 0.0 us)
Async XLA Ops:
  0.0 6.3 %collective-permute-start.1 = (f32[2,64,512]{2,1,0:T(8,128)}, f32[2,64,512]{2,1,0:T(8,128)S(1)}, u32[]{:S(2)}, u32[]{:S(2)}) collective-permute-start(f32[2,64,512]{2,1,0:T(8,128)} %param.9), channel_id=1, source_target_pairs={{0,1},{1,0},{2,3},{3,2},{4,5},{5,4},{6,7},{7,6},{8,9},{9,8},{10,11... | collective-permute-start | bytes 786440 | tf_op jit(solution)/shard_map/ppermute | solution.py:18
  1.2 9.5 %copy-start = (f32[128,512]{1,0:T(8,128)S(1)}, f32[128,512]{1,0:T(8,128)}, u32[]{:S(2)}) copy-start(f32[128,512]{1,0:T(8,128)} %constant.21.clone.rows_ref) | copy-start | bytes 786436
  1.2 5.1 %collective-permute-start = (f32[4,512]{1,0:T(4,128)S(1)}, f32[4,512]{1,0:T(4,128)S(1)}, u32[]{:S(2)}, u32[]{:S(2)}) collective-permute-start(f32[4,512]{1,0:T(4,128)S(1)} %pack.1.refs_1_), channel_id=1, source_target_pairs={{0,9},{1,8},{2,11},{3,10},{4,13},{5,12},{6,15},{7,14},{8,1},{9,0},... | collective-permute-start | bytes 24584 | tf_op jit(solution)/shard_map/ppermute | solution.py:18
  6.5 1.2 %collective-permute-start.2 = (f32[2,3,128]{2,1,0:T(4,128)S(1)}, f32[2,3,128]{2,1,0:T(4,128)S(1)}, u32[]{:S(2)}, u32[]{:S(2)}) collective-permute-start(f32[2,3,128]{2,1,0:T(4,128)S(1)} %anti_totals.1), channel_id=1, source_target_pairs={{0,1},{1,0},{2,3},{3,2},{4,5},{5,4},{6,7},{7,6},{8,9},{9,8},{10,11... | collective-permute-start | bytes 9224 | tf_op jit(solution)/shard_map/ppermute | solution.py:18
  7.7 4.8 %collective-permute-start.5 = (f32[2,3,128]{2,1,0:T(4,128)S(1)}, f32[2,3,128]{2,1,0:T(4,128)S(1)}, u32[]{:S(2)}, u32[]{:S(2)}) collective-permute-start(f32[2,3,128]{2,1,0:T(4,128)S(1)} %add.97.refs_2_.after_ref), channel_id=1, source_target_pairs={{0,7},{1,6},{2,5},{3,4},{4,3},{5,2},{6,1},{7,0},{8,15},{9,14},{10,... | collective-permute-start | bytes 9224 | tf_op jit(solution)/shard_map/ppermute | solution.py:18
  10.2 3.0 %collective-permute-start.4 = (f32[2,3,128]{2,1,0:T(4,128)S(1)}, f32[2,3,128]{2,1,0:T(4,128)S(1)}, u32[]{:S(2)}, u32[]{:S(2)}) collective-permute-start(f32[2,3,128]{2,1,0:T(4,128)S(1)} %add.97.refs_2_.after_ref), channel_id=1, source_target_pairs={{0,5},{1,4},{2,7},{3,6},{4,1},{5,0},{6,3},{7,2},{8,13},{9,12},{10,... | collective-permute-start | bytes 9224 | tf_op jit(solution)/shard_map/ppermute | solution.py:18
  10.5 3.0 %collective-permute-start.3 = (f32[2,3,128]{2,1,0:T(4,128)S(1)}, f32[2,3,128]{2,1,0:T(4,128)S(1)}, u32[]{:S(2)}, u32[]{:S(2)}) collective-permute-start(f32[2,3,128]{2,1,0:T(4,128)S(1)} %add.97.refs_2_.after_ref), channel_id=1, source_target_pairs={{0,3},{1,2},{2,1},{3,0},{4,7},{5,6},{6,5},{7,4},{8,11},{9,10},{10,... | collective-permute-start | bytes 9224 | tf_op jit(solution)/shard_map/ppermute | solution.py:18
  12.5 5.1 %copy-start.1 = (bf16[128,512]{1,0:T(8,128)(2,1)S(1)}, bf16[128,512]{1,0:T(8,128)(2,1)}, u32[]{:S(2)}) copy-start(bf16[128,512]{1,0:T(8,128)(2,1)} %constant.20.clone.basis_ref) | copy-start | bytes 393220
  13.6 4.0 %collective-permute-start.6 = (f32[3,3,128]{2,1,0:T(4,128)S(1)}, f32[3,3,128]{2,1,0:T(4,128)S(1)}, u32[]{:S(2)}, u32[]{:S(2)}) collective-permute-start(f32[3,3,128]{2,1,0:T(4,128)S(1)} %pad_maximum_fusion), channel_id=1, source_target_pairs={{0,9},{1,8},{2,11},{3,10},{4,13},{5,12},{6,15},{7,14},{8,1},{9,0},... | collective-permute-start | bytes 13832 | tf_op jit(solution)/shard_map/ppermute | solution.py:18

commit v8 on v7

--- a/solution.py
+++ b/solution.py
@@ -81,7 +81,7 @@
             part_ref[k, moment : moment + 1] = sums[moment][1 + k : 2 + k]
 
 
-def spectrum_kernel(index_ref, rows_ref, arm_ref, after_ref, spec_ref, arms_ref):
+def spectrum_kernel(index_ref, rows_ref, arm_ref, after_ref, basis_ref, spec_ref, arms_ref):
     for row in range(2):
         for s in range(arms_ref.shape[1]):
             arms_ref[row, s : s + 1] = jnp.broadcast_to(arm_ref[row : row + 1, s : s + 1], (1, arms_ref.shape[2]))
@@ -180,7 +180,7 @@
     )(in_vmem(far_geom), in_vmem(near_anti), in_vmem(total))
     spec, arm = pl.pallas_call(
         spectrum_kernel, out_shape=(pltpu.VMEM((gusts, wide), f32), pltpu.VMEM((2, s_dev, wide), f32)), name="spectrum"
-    )(gust_index.reshape(1, gusts), in_vmem(jnp.asarray(rows)), station_geom, in_vmem(total))
+    )(gust_index.reshape(1, gusts), in_vmem(jnp.asarray(rows)), station_geom, in_vmem(total), in_vmem(basis))
     low, high = 1, half.bit_length() - 1
     while low < high:
         size = min(2, high - low)

time: 19 us -> 19 us (level)
  no operation moved by 1% of the time
where the time goes in v8:
time: 19 us; the launch traced here: 18.8 us
  starting transfers between devices  9.9 us (52%)
  Pallas kernels  5.1 us (27%)
  waiting for transfers between devices  3.66 us (19%)
    ppermute x7, starting transfers between devices, swap(): return lax.ppermute(block, axis, [(i, i ^ mask) for i in range(count)])  9.9 us
    ppermute x7, waiting for transfers between devices, swap(): return lax.ppermute(block, axis, [(i, i ^ mask) for i in range(count)])  3.66 us
    pallas_call x1, Pallas kernels, on_device(): pl.pallas_call(spectrum_kernel, out_shape=(pltpu.VMEM((gusts, wide), f32)...  1.58 us
    pallas_call x1, Pallas kernels, on_device(): pl.pallas_call(lambda *refs: sym_kernel(s_dev, *refs), out_shape=(pltpu.V...  1.19 us
    pallas_call x1, Pallas kernels, on_device(): pl.pallas_call(history_kernel, out_shape=jax.ShapeDtypeStruct((s_dev * 6...  1.17 us
    pallas_call x1, Pallas kernels, on_device(): pl.pallas_call(pack_kernel, out_shape=pltpu.VMEM((4, box_dev), f32), name...  0.71 us
  transfers between devices with their start and end apart: 7, of which 5 were waited for; matrix products, arithmetic and copies ran while one was open for 0% of the time, Pallas kernels for 20%

profile of v8, /device:TPU:0, one launch (start us, length us, event | category | flops | bytes accessed | tf_op | source)
XLA Modules:
  0.0 18.8 jit_solution(9771936013588311490)
XLA Ops:
  0.0 0.5 %collective-permute-start.1 = (f32[2,64,512]{2,1,0:T(8,128)}, f32[2,64,512]{2,1,0:T(8,128)S(1)}, u32[]{:S(2)}, u32[]{:S(2)}) collective-permute-start(f32[2,64,512]{2,1,0:T(8,128)} %param.9), channel_id=1, source_target_pairs={{0,1},{1,0},{2,3},{3,2},{4,5},{5,4},{6,7},{7,6},{8,9},{9,8},{10,11... | collective-permute-start | bytes 786440 | tf_op jit(solution)/shard_map/ppermute | solution.py:18
  0.5 0.7 %pack.1.refs_1_ = f32[4,512]{1,0:T(4,128)S(1)} custom-call(f32[3,512]{1,0:T(4,128)} %geom_ref.1, s32[4,128]{1,0:T(4,128)} %bitcast.17), custom_call_target="tpu_custom_call" | custom-call | tf_op jit(solution)/shard_map/pack/pallas_call | solution.py:153
  1.2 0.0 copy-start.1
  1.2 3.8 %collective-permute-start = (f32[4,512]{1,0:T(4,128)S(1)}, f32[4,512]{1,0:T(4,128)S(1)}, u32[]{:S(2)}, u32[]{:S(2)}) collective-permute-start(f32[4,512]{1,0:T(4,128)S(1)} %pack.1.refs_1_), channel_id=1, source_target_pairs={{0,9},{1,8},{2,11},{3,10},{4,13},{5,12},{6,15},{7,14},{8,1},{9,0},... | collective-permute-start | bytes 24584 | tf_op jit(solution)/shard_map/ppermute | solution.py:18
  4.9 1.2 %sym_sums.1 = (f32[3,128]{1,0:T(4,128)S(1)}, f32[2,3,128]{2,1,0:T(4,128)S(1)}) custom-call(f32[2,64,512]{2,1,0:T(8,128)} %refs_0_.1, f32[4,512]{1,0:T(4,128)S(1)} %pack.1.refs_1_), custom_call_target="tpu_custom_call" | custom-call | tf_op jit(solution)/shard_map/sym_sums/pallas_call | solution.py:156
  6.1 0.2 collective-permute-done.geom_ref.refs_0_
  6.3 0.0 collective-permute-done.1.anti_ref.refs_1_
  6.3 0.0 copy-start
  6.3 0.2 %anti_totals.1 = f32[2,3,128]{2,1,0:T(4,128)S(1)} custom-call(f32[4,512]{1,0:T(4,128)S(1)} %collective-permute-done.geom_ref.refs_0_, f32[2,64,512]{2,1,0:T(8,128)S(1)} %collective-permute-done.1.anti_ref.refs_1_, f32[3,128]{1,0:T(4,128)S(1)} %get-tuple-element.13.sym_ref), custom_call_target="tpu_custom_call" | custom-call | tf_op jit(solution)/shard_map/anti_totals/pallas_call | solution.py:161
  6.5 0.1 collective-permute-start.2
  6.6 1.1 %collective-permute-done.2 = f32[2,3,128]{2,1,0:T(4,128)S(1)} collective-permute-done((f32[2,3,128]{2,1,0:T(4,128)S(1)}, f32[2,3,128]{2,1,0:T(4,128)S(1)}, u32[]{:S(2)}, u32[]{:S(2)}) %collective-permute-start.2) | collective-permute-done | bytes 3104 | tf_op jit(solution)/shard_map/ppermute | solution.py:18
  7.7 2.6 %collective-permute-start.5 = (f32[2,3,128]{2,1,0:T(4,128)S(1)}, f32[2,3,128]{2,1,0:T(4,128)S(1)}, u32[]{:S(2)}, u32[]{:S(2)}) collective-permute-start(f32[2,3,128]{2,1,0:T(4,128)S(1)} %add.97.refs_2_.after_ref), channel_id=1, source_target_pairs={{0,7},{1,6},{2,5},{3,4},{4,3},{5,2},{6,1},{7,0},{8,15},{9,14},{10,... | collective-permute-start | bytes 9224 | tf_op jit(solution)/shard_map/ppermute | solution.py:18
  10.3 0.2 %collective-permute-start.4 = (f32[2,3,128]{2,1,0:T(4,128)S(1)}, f32[2,3,128]{2,1,0:T(4,128)S(1)}, u32[]{:S(2)}, u32[]{:S(2)}) collective-permute-start(f32[2,3,128]{2,1,0:T(4,128)S(1)} %add.97.refs_2_.after_ref), channel_id=1, source_target_pairs={{0,5},{1,4},{2,7},{3,6},{4,1},{5,0},{6,3},{7,2},{8,13},{9,12},{10,... | collective-permute-start | bytes 9224 | tf_op jit(solution)/shard_map/ppermute | solution.py:18
  10.5 0.2 %collective-permute-start.3 = (f32[2,3,128]{2,1,0:T(4,128)S(1)}, f32[2,3,128]{2,1,0:T(4,128)S(1)}, u32[]{:S(2)}, u32[]{:S(2)}) collective-permute-start(f32[2,3,128]{2,1,0:T(4,128)S(1)} %add.97.refs_2_.after_ref), channel_id=1, source_target_pairs={{0,3},{1,2},{2,1},{3,0},{4,7},{5,6},{6,5},{7,4},{8,11},{9,10},{10,... | collective-permute-start | bytes 9224 | tf_op jit(solution)/shard_map/ppermute | solution.py:18
  10.7 0.0 copy-done.1
  10.7 0.0 copy-done
  10.7 1.6 %spectrum.1 = (f32[64,128]{1,0:T(8,128)S(1)}, f32[2,2,128]{2,1,0:T(2,128)S(1)}) custom-call(s32[1,64]{1,0:T(1,128)} %bitcast.18, f32[128,512]{1,0:T(8,128)S(1)} %copy-done.1, f32[2,2]{1,0:T(2,128)} %arm_ref.1, f32[2,3,128]{2,1,0:T(4,128)S(1)} %add.97.refs_2_.after_ref, bf16[128,512]{1,0:T(8,128)(2,1)S(1)} %copy-done), custom_call_target="tpu_custom_call" | custom-call | tf_op jit(solution)/shard_map/spectrum/pallas_call | solution.py:181
  12.3 0.2 %anti_parts.1 = f32[2,3,128]{2,1,0:T(4,128)S(1)} custom-call(f32[4,512]{1,0:T(4,128)S(1)} %collective-permute-done.geom_ref.refs_0_, f32[2,64,512]{2,1,0:T(8,128)S(1)} %collective-permute-done.1.anti_ref.refs_1_, f32[2,3,128]{2,1,0:T(4,128)S(1)} %add.97.refs_2_.after_ref), custom_call_target="tpu_custom_call" | custom-call | tf_op jit(solution)/shard_map/anti_parts/pallas_call | solution.py:176
  12.5 0.0 collective-permute-done.5
  12.5 0.8 %collective-permute-done.4 = f32[2,3,128]{2,1,0:T(4,128)S(1)} collective-permute-done((f32[2,3,128]{2,1,0:T(4,128)S(1)}, f32[2,3,128]{2,1,0:T(4,128)S(1)}, u32[]{:S(2)}, u32[]{:S(2)}) %collective-permute-start.4) | collective-permute-done | bytes 3104 | tf_op jit(solution)/shard_map/ppermute | solution.py:18
  13.3 0.2 %collective-permute-done.3 = f32[2,3,128]{2,1,0:T(4,128)S(1)} collective-permute-done((f32[2,3,128]{2,1,0:T(4,128)S(1)}, f32[2,3,128]{2,1,0:T(4,128)S(1)}, u32[]{:S(2)}, u32[]{:S(2)}) %collective-permute-start.3) | collective-permute-done | bytes 3104 | tf_op jit(solution)/shard_map/ppermute | solution.py:18
  13.6 2.6 %collective-permute-start.6 = (f32[3,3,128]{2,1,0:T(4,128)S(1)}, f32[3,3,128]{2,1,0:T(4,128)S(1)}, u32[]{:S(2)}, u32[]{:S(2)}) collective-permute-start(f32[3,3,128]{2,1,0:T(4,128)S(1)} %pad_maximum_fusion), channel_id=1, source_target_pairs={{0,9},{1,8},{2,11},{3,10},{4,13},{5,12},{6,15},{7,14},{8,1},{9,0},... | collective-permute-start | bytes 13832 | tf_op jit(solution)/shard_map/ppermute | solution.py:18
  16.2 1.4 %collective-permute-done.6 = f32[3,3,128]{2,1,0:T(4,128)S(1)} collective-permute-done((f32[3,3,128]{2,1,0:T(4,128)S(1)}, f32[3,3,128]{2,1,0:T(4,128)S(1)}, u32[]{:S(2)}, u32[]{:S(2)}) %collective-permute-start.6) | collective-permute-done | bytes 4640 | tf_op jit(solution)/shard_map/ppermute | solution.py:18
  17.6 1.2 %histories.1 = bf16[768,512]{1,0:T(8,128)(2,1)} custom-call(f32[2,3,128]{2,1,0:T(4,128)S(1)} %get-tuple-element.27.sym_ref, f32[2,3,128]{2,1,0:T(4,128)S(1)} %get-tuple-element.26.anti_ref, f32[2,2,128]{2,1,0:T(2,128)S(1)} %get-tuple-element.17.arm_ref, f32[64,128]{1,0:T(8,128)S(1)} %get-tuple-element.18.spec_ref, bf16[128,512]{1,0:T(8,128)(2,1)S(1)} %copy-done), custom_call_target="tpu_custom_call" | custom-call | tf_op jit(solution)/shard_map/histories/pallas_call | solution.py:200
  (8 shorter events, 0.0 us)
Async XLA Ops:
  0.0 6.3 %collective-permute-start.1 = (f32[2,64,512]{2,1,0:T(8,128)}, f32[2,64,512]{2,1,0:T(8,128)S(1)}, u32[]{:S(2)}, u32[]{:S(2)}) collective-permute-start(f32[2,64,512]{2,1,0:T(8,128)} %param.9), channel_id=1, source_target_pairs={{0,1},{1,0},{2,3},{3,2},{4,5},{5,4},{6,7},{7,6},{8,9},{9,8},{10,11... | collective-permute-start | bytes 786440 | tf_op jit(solution)/shard_map/ppermute | solution.py:18
  1.2 9.5 %copy-start.1 = (f32[128,512]{1,0:T(8,128)S(1)}, f32[128,512]{1,0:T(8,128)}, u32[]{:S(2)}) copy-start(f32[128,512]{1,0:T(8,128)} %constant.21.clone.rows_ref) | copy-start | bytes 786436
  1.2 5.1 %collective-permute-start = (f32[4,512]{1,0:T(4,128)S(1)}, f32[4,512]{1,0:T(4,128)S(1)}, u32[]{:S(2)}, u32[]{:S(2)}) collective-permute-start(f32[4,512]{1,0:T(4,128)S(1)} %pack.1.refs_1_), channel_id=1, source_target_pairs={{0,9},{1,8},{2,11},{3,10},{4,13},{5,12},{6,15},{7,14},{8,1},{9,0},... | collective-permute-start | bytes 24584 | tf_op jit(solution)/shard_map/ppermute | solution.py:18
  6.3 4.4 %copy-start = (bf16[128,512]{1,0:T(8,128)(2,1)S(1)}, bf16[128,512]{1,0:T(8,128)(2,1)}, u32[]{:S(2)}) copy-start(bf16[128,512]{1,0:T(8,128)(2,1)} %constant.20.clone.basis_ref) | copy-start | bytes 393220
  6.5 1.2 %collective-permute-start.2 = (f32[2,3,128]{2,1,0:T(4,128)S(1)}, f32[2,3,128]{2,1,0:T(4,128)S(1)}, u32[]{:S(2)}, u32[]{:S(2)}) collective-permute-start(f32[2,3,128]{2,1,0:T(4,128)S(1)} %anti_totals.1), channel_id=1, source_target_pairs={{0,1},{1,0},{2,3},{3,2},{4,5},{5,4},{6,7},{7,6},{8,9},{9,8},{10,11... | collective-permute-start | bytes 9224 | tf_op jit(solution)/shard_map/ppermute | solution.py:18
  7.7 4.8 %collective-permute-start.5 = (f32[2,3,128]{2,1,0:T(4,128)S(1)}, f32[2,3,128]{2,1,0:T(4,128)S(1)}, u32[]{:S(2)}, u32[]{:S(2)}) collective-permute-start(f32[2,3,128]{2,1,0:T(4,128)S(1)} %add.97.refs_2_.after_ref), channel_id=1, source_target_pairs={{0,7},{1,6},{2,5},{3,4},{4,3},{5,2},{6,1},{7,0},{8,15},{9,14},{10,... | collective-permute-start | bytes 9224 | tf_op jit(solution)/shard_map/ppermute | solution.py:18
  10.3 3.0 %collective-permute-start.4 = (f32[2,3,128]{2,1,0:T(4,128)S(1)}, f32[2,3,128]{2,1,0:T(4,128)S(1)}, u32[]{:S(2)}, u32[]{:S(2)}) collective-permute-start(f32[2,3,128]{2,1,0:T(4,128)S(1)} %add.97.refs_2_.after_ref), channel_id=1, source_target_pairs={{0,5},{1,4},{2,7},{3,6},{4,1},{5,0},{6,3},{7,2},{8,13},{9,12},{10,... | collective-permute-start | bytes 9224 | tf_op jit(solution)/shard_map/ppermute | solution.py:18
  10.5 3.0 %collective-permute-start.3 = (f32[2,3,128]{2,1,0:T(4,128)S(1)}, f32[2,3,128]{2,1,0:T(4,128)S(1)}, u32[]{:S(2)}, u32[]{:S(2)}) collective-permute-start(f32[2,3,128]{2,1,0:T(4,128)S(1)} %add.97.refs_2_.after_ref), channel_id=1, source_target_pairs={{0,3},{1,2},{2,1},{3,0},{4,7},{5,6},{6,5},{7,4},{8,11},{9,10},{10,... | collective-permute-start | bytes 9224 | tf_op jit(solution)/shard_map/ppermute | solution.py:18
  13.6 4.0 %collective-permute-start.6 = (f32[3,3,128]{2,1,0:T(4,128)S(1)}, f32[3,3,128]{2,1,0:T(4,128)S(1)}, u32[]{:S(2)}, u32[]{:S(2)}) collective-permute-start(f32[3,3,128]{2,1,0:T(4,128)S(1)} %pad_maximum_fusion), channel_id=1, source_target_pairs={{0,9},{1,8},{2,11},{3,10},{4,13},{5,12},{6,15},{7,14},{8,1},{9,0},... | collective-permute-start | bytes 13832 | tf_op jit(solution)/shard_map/ppermute | solution.py:18
